TPU v7x, 32 devices: a whole 2x2x4 slice. The times are simulated.
32 devices in a mesh: section: 2 (over x), batch: 16 (over z, y, core).
Axes of the slice: x: 2, y: 2, z: 4, core: 2. Of those that a mesh axis runs over, the one named last changes fastest.
Arguments:
- patches: bfloat16 [8192, 768], P('batch'), may hold values from -6 to 6
- code_signs: int32 [8192, 18], P('batch'), may hold values from 0 to 1
- tile_ids: int32 [32, 256], P('batch'), may hold values from 0 to 2, never falling along the last dimension, each value on 1 to 128 neighbouring positions
- patch_valid: int32 [32, 256], P('batch'), may hold values 0 or 1
- cotangent: bfloat16 [8192, 768], P('batch'), may hold values from -6 to 6
- attend_weight: bfloat16 [2, 768, 2304], P('section'), may hold values from -0.21875 to 0.21875
- project_weight: bfloat16 [2, 768, 768], P('section'), may hold values from -1.75 to 1.75
- expand_weight: bfloat16 [2, 768, 3072], P('section'), may hold values from -0.21875 to 0.21875
- shrink_weight: bfloat16 [2, 3072, 768], P('section'), may hold values from -0.15625 to 0.15625
- norm_first: float32 [2, 768], P('section'), may hold values from 0.1 to 1.9
- norm_second: float32 [2, 768], P('section'), may hold values from 0.1 to 1.9
- bottleneck: bfloat16 [2, 768, 18], P('section'), may hold values from -6 to 6
Outputs:
- results: bfloat16 [2, 8192, 768], P('section', 'batch')
- grad_attend: float32 [2, 768, 2304], P('section', 'batch')
- grad_project: float32 [2, 768, 768], P('section', 'batch')
- grad_expand: float32 [2, 768, 3072], P('section', 'batch')
- grad_shrink: float32 [2, 3072, 768], P('section', 'batch')
- grad_first: float32 [2, 768], P('section', 'batch')
- grad_second: float32 [2, 768], P('section', 'batch')
- grad_bottleneck: float32 [2, 768, 18], P('section', 'batch')
Inputs may be any that keep to these rules, and one draw needn't show every extreme that they name: `tile_ids`: within each image the tile numbers never fall; each tile covers 1 to 128 slots, and one tile of each image covers exactly 128.
All inputs are finite; a program needn't handle non-finite values. No bound on the sum of `patch_valid` on one device may be relied on, other than what follows from the above.
Results may differ from a plain program's by a relative error of at most 0.02.
Values may be sent and summed in bfloat16 or wider, within the bound.
A program may use at most 256 MiB of HBM per device.

v0:
```python
import functools
import math

import jax
import jax.numpy as jnp
from jax import lax
from jax.experimental import pallas as pl
from jax.experimental.pallas import tpu as pltpu
from jax.sharding import PartitionSpec as P

H = 12
HD = 64
MESH = pl.DeviceIdType.MESH
ROWS = 48


def passed_along(block, axis, distance):
    devices = range(lax.axis_size(axis))
    route = [(i - distance, i) for i in devices if i - distance in devices]
    return lax.ppermute(block, axis, route)


def contract_rows(former, latter):
    return lax.dot_general(
        former, latter, (((0,), (0,)), ((), ())), preferred_element_type=jnp.float32
    )


def times_transpose(former, latter):
    return lax.dot_general(
        former, latter, (((1,), (1,)), ((), ())), preferred_element_type=jnp.float32
    )


def normalize(values):
    average = jnp.mean(values, axis=-1, keepdims=True)
    center = values - average
    spread = jnp.mean(center * center, axis=-1, keepdims=True)
    factor = lax.rsqrt(spread + 1e-06)
    return (center * factor, factor)


def norm_back(grad_normed, normed, factor):
    return factor * (
        grad_normed
        - jnp.mean(grad_normed, axis=-1, keepdims=True)
        - normed * jnp.mean(grad_normed * normed, axis=-1, keepdims=True)
    )


def allowed(tile_row, keep_row):
    places = jnp.arange(tile_row.shape[0])
    same_tile = tile_row[:, None] == tile_row[None, :]
    live_keys = keep_row[None, :] == 1
    return same_tile & live_keys | (places[:, None] == places[None, :])


def block_forward(residual, weights, allowed_keys):
    attend, project, expand, shrink, first, second = weights
    length, model_width = residual.shape
    normed_one, factor_one = normalize(residual)
    input_one = (normed_one * first).astype(jnp.bfloat16)
    joint_proj = jnp.dot(input_one, attend, preferred_element_type=jnp.float32).astype(jnp.bfloat16)
    split_parts = joint_proj.reshape(length, 3, H, HD)
    queries = split_parts[:, 0]
    key_rows = split_parts[:, 1]
    value_rows = split_parts[:, 2]
    scores = jnp.einsum(
        "qhd,khd->hqk", queries, key_rows, preferred_element_type=jnp.float32
    ) * HD ** (-0.5)
    scores = jnp.where(allowed_keys[None], scores, -1000000000.0)
    maximum = jnp.max(scores, axis=-1, keepdims=True)
    raised = jnp.exp(scores - maximum)
    softmax_out = raised / jnp.sum(raised, axis=-1, keepdims=True)
    softmax_low = softmax_out.astype(jnp.bfloat16)
    mixed_heads = jnp.einsum(
        "hqk,khd->qhd", softmax_low, value_rows, preferred_element_type=jnp.float32
    )
    mixed_heads = mixed_heads.reshape(length, model_width).astype(jnp.bfloat16)
    middle = residual + jnp.dot(mixed_heads, project, preferred_element_type=jnp.float32)
    normed_two, factor_two = normalize(middle)
    input_two = (normed_two * second).astype(jnp.bfloat16)
    hidden = jnp.dot(input_two, expand, preferred_element_type=jnp.float32)
    active = jax.nn.gelu(hidden, approximate=False).astype(jnp.bfloat16)
    output = middle + jnp.dot(active, shrink, preferred_element_type=jnp.float32)
    kept_parts = (
        normed_one,
        factor_one,
        input_one,
        queries,
        key_rows,
        value_rows,
        softmax_out,
        softmax_low,
        mixed_heads,
        normed_two,
        factor_two,
        input_two,
        hidden,
        active,
    )
    return (output, kept_parts)


def block_backward(kept_parts, grad_out, weights):
    attend, project, expand, shrink, first, second = weights
    (
        normed_one,
        factor_one,
        input_one,
        queries,
        key_rows,
        value_rows,
        softmax_out,
        softmax_low,
        mixed_heads,
        normed_two,
        factor_two,
        input_two,
        hidden,
        active,
    ) = kept_parts
    length, model_width = grad_out.shape
    grad_rounded = grad_out.astype(jnp.bfloat16)
    grad_shrink = contract_rows(active, grad_rounded)
    grad_active = times_transpose(grad_rounded, shrink)
    _, gelu_back = jax.vjp(lambda values: jax.nn.gelu(values, approximate=False), hidden)
    grad_hidden = gelu_back(grad_active)[0].astype(jnp.bfloat16)
    grad_expand = contract_rows(input_two, grad_hidden)
    grad_input_two = times_transpose(grad_hidden, expand)
    grad_second = jnp.sum(grad_input_two * normed_two, axis=0)
    grad_middle = grad_out + norm_back(grad_input_two * second, normed_two, factor_two)
    middle_low = grad_middle.astype(jnp.bfloat16)
    grad_project = contract_rows(mixed_heads, middle_low)
    grad_mixed = times_transpose(middle_low, project).astype(jnp.bfloat16).reshape(length, H, HD)
    grad_soft = jnp.einsum(
        "qhd,khd->hqk", grad_mixed, value_rows, preferred_element_type=jnp.float32
    )
    grad_values = jnp.einsum(
        "hqk,qhd->khd", softmax_low, grad_mixed, preferred_element_type=jnp.float32
    )
    inner_sum = jnp.sum(softmax_out * grad_soft, axis=-1, keepdims=True)
    grad_scores = (softmax_out * (grad_soft - inner_sum)).astype(jnp.bfloat16)
    score_scale = HD ** (-0.5)
    grad_queries = (
        jnp.einsum("hqk,khd->qhd", grad_scores, key_rows, preferred_element_type=jnp.float32)
        * score_scale
    )
    grad_keys = (
        jnp.einsum("hqk,qhd->khd", grad_scores, queries, preferred_element_type=jnp.float32)
        * score_scale
    )
    grad_joint = (
        jnp.stack([grad_queries, grad_keys, grad_values], axis=1)
        .reshape(length, 3 * model_width)
        .astype(jnp.bfloat16)
    )
    grad_attend = contract_rows(input_one, grad_joint)
    grad_input_one = times_transpose(grad_joint, attend)
    grad_first = jnp.sum(grad_input_one * normed_one, axis=0)
    grad_residual = grad_middle + norm_back(grad_input_one * first, normed_one, factor_one)
    return (
        grad_residual,
        (grad_attend, grad_project, grad_expand, grad_shrink, grad_first, grad_second),
    )


def rows_of(index):
    return pl.ds(pl.multiple_of(index * ROWS, ROWS), ROWS)


def place(z, y, core, depth):
    return (core * 2 + y) * depth + z


class Reduction:
    def __init__(self, depth, parts, total, scratch):
        self.depth = depth
        self.parts, self.total = parts, total
        self.from_core, self.from_y, self.from_low, self.from_high = scratch[:4]
        self.core_s, self.core_r, self.y_s, self.y_r = scratch[4:8]
        self.up_s, self.up_r, self.down_s, self.down_r = scratch[8:12]
        self.section = lax.axis_index("section")
        self.me = lax.axis_index("batch")
        self.z, self.y, self.core = self.me // 4, (self.me // 2) % 2, self.me % 2

    def scratch(depth, count, wide):
        return (
            [pltpu.VMEM((count, 2 * depth * ROWS, wide), jnp.bfloat16)]
            + [pltpu.VMEM((count, depth * ROWS, wide), jnp.bfloat16)]
            + [pltpu.VMEM((count, (depth - 1) * ROWS, wide), jnp.bfloat16)] * 2
            + [pltpu.SemaphoreType.DMA((count,))] * 4
            + [pltpu.SemaphoreType.DMA((count, depth))] * 4
        )

    def peers(self):
        def device(z, y, core):
            return (self.section, z * 4 + y * 2 + core)

        return (
            device(self.z, self.y, 1 - self.core),
            device(self.z, 1 - self.y, self.core),
            device(jnp.minimum(self.z + 1, self.depth - 1), self.y, self.core),
            device(jnp.maximum(self.z - 1, 0), self.y, self.core),
            (1 - self.section, self.me),
        )

    def greet(self):
        barrier = pltpu.get_barrier_semaphore()
        core, other, high, low, across = self.peers()

        def signal(device):
            pl.semaphore_signal(barrier, inc=1, device_id=device, device_id_type=MESH)

        signal(core)
        signal(other)
        signal(across)

        @pl.when(self.z < self.depth - 1)
        def _():
            signal(high)

        @pl.when(self.z > 0)
        def _():
            signal(low)

        ends = (self.z == 0) | (self.z == self.depth - 1)

        @pl.when(ends)
        def _():
            pl.semaphore_wait(barrier, 4)

        @pl.when(jnp.logical_not(ends))
        def _():
            pl.semaphore_wait(barrier, 5)

    def block(self, k, core, y, z):
        return self.parts.at[k, rows_of(place(z, y, core, self.depth))]

    def core_copy(self, k):
        half = 2 * self.depth * ROWS
        return pltpu.make_async_remote_copy(
            self.parts.at[k, pl.ds(pl.multiple_of((1 - self.core) * half, half), half)],
            self.from_core.at[k], self.core_s.at[k], self.core_r.at[k],
            device_id=self.peers()[0], device_id_type=MESH,
        )

    def y_copy(self, k):
        quarter = self.depth * ROWS
        start = (self.core * 2 + 1 - self.y) * quarter
        return pltpu.make_async_remote_copy(
            self.parts.at[k, pl.ds(pl.multiple_of(start, quarter), quarter)],
            self.from_y.at[k], self.y_s.at[k], self.y_r.at[k],
            device_id=self.peers()[1], device_id_type=MESH,
        )

    def up_copy(self, k, to):
        return pltpu.make_async_remote_copy(
            self.block(k, self.core, self.y, to), self.from_low.at[k, rows_of(to - 1)],
            self.up_s.at[k, to], self.up_r.at[k, to],
            device_id=self.peers()[2], device_id_type=MESH,
        )

    def down_copy(self, k, to):
        return pltpu.make_async_remote_copy(
            self.block(k, self.core, self.y, to), self.from_high.at[k, rows_of(to)],
            self.down_s.at[k, to], self.down_r.at[k, to],
            device_id=self.peers()[3], device_id_type=MESH,
        )

    def add(self, here, other):
        here[...] = (here[...].astype(jnp.float32) + other.astype(jnp.float32)).astype(jnp.bfloat16)

    def start(self, k):
        self.core_copy(k).start()

    def after_core(self, k):
        self.core_copy(k).wait_recv()
        for far in (1, 0):
            half = (self.y + far) % 2

            @pl.loop(0, self.depth)
            def _(to):
                self.add(self.block(k, self.core, half, to), self.from_core[k, rows_of(half * self.depth + to)])

            if far:
                self.y_copy(k).start()

    def after_y(self, k):
        self.y_copy(k).wait_recv()

        @pl.loop(0, self.depth)
        def _(to):
            self.add(self.block(k, self.core, self.y, to), self.from_y[k, rows_of(to)])

    def go_up(self, k):
        for to in range(self.depth - 1, 0, -1):

            @pl.when(self.z < to)
            def _():
                copy = self.up_copy(k, to)

                @pl.when(self.z > 0)
                def _():
                    copy.wait_recv()
                    self.add(self.block(k, self.core, self.y, to), self.from_low[k, rows_of(to - 1)])

                copy.start()

    def go_down(self, k):
        for to in range(self.depth - 1):

            @pl.when(self.z > to)
            def _():
                copy = self.down_copy(k, to)

                @pl.when(self.z < self.depth - 1)
                def _():
                    copy.wait_recv()
                    self.add(self.block(k, self.core, self.y, to), self.from_high[k, rows_of(to)])

                copy.start()

    def finish(self, k):
        own = self.block(k, self.core, self.y, self.z)
        low = self.from_low.at[k, rows_of(jnp.maximum(self.z - 1, 0))]
        high = self.from_high.at[k, rows_of(jnp.minimum(self.z, self.depth - 2))]

        @pl.when(self.z == 0)
        def _():
            self.down_copy(k, self.z).wait_recv()
            self.total[k] = own[...].astype(jnp.float32) + high[...].astype(jnp.float32)

        @pl.when(self.z == self.depth - 1)
        def _():
            self.up_copy(k, self.z).wait_recv()
            self.total[k] = own[...].astype(jnp.float32) + low[...].astype(jnp.float32)

        @pl.when((self.z > 0) & (self.z < self.depth - 1))
        def _():
            self.down_copy(k, self.z).wait_recv()
            self.up_copy(k, self.z).wait_recv()
            self.total[k] = (
                own[...].astype(jnp.float32) + high[...].astype(jnp.float32) + low[...].astype(jnp.float32)
            )

    def drain(self, k):
        self.core_copy(k).wait_send()
        self.y_copy(k).wait_send()
        for to in range(self.depth - 1):

            @pl.when(self.z < to + 1)
            def _():
                self.up_copy(k, to + 1).wait_send()

            @pl.when(self.z > to)
            def _():
                self.down_copy(k, to).wait_send()

    def along(self, t, count):
        last = self.depth - 1
        at(t, count, self.after_y)
        at(t - self.z, count, self.go_up)
        at(t - last + self.z, count, self.go_down)
        at(t - 1 - last, count, self.finish)


def at(k, count, action):
    @pl.when((k >= 0) & (k < count))
    def _():
        action(k)


def over(count, size):
    def run(action):
        @pl.loop(0, count // size)
        def _(i):
            action(pl.ds(pl.multiple_of(i * size, size), size))

    return run


def train_kernel(
    depth, images,
    patches, signs, tiles, valid, cotangent, attend_in, project_in, expand_in, shrink_in, first, second, bottle_in,
    results, total, rest,
    parts, attend, project, left, right, soft, temp, saved, normed_one, normed_two, residual, work, factor_one,
    factor_two, bias, codes, bottle, delta, code_grad, bottle_sum, gain_one, gain_two, extra,
    loads, code_sems, *scratch,
):
    rows, width = patches.shape
    length = rows // images
    count, slabs = parts.shape[0], shrink_in.shape[0] // width
    pairs = width // 128
    main = Reduction(depth, parts, total, scratch[:12])
    small = Reduction(depth, extra, rest, scratch[12:24])
    encoding = main.section == 0
    lane = lax.broadcasted_iota(jnp.int32, (length, 128), 1)
    low_half = lane < HD
    bf, f32 = jnp.bfloat16, jnp.float32

    def dot(a, b):
        return jnp.dot(a, b, preferred_element_type=f32)

    def load(source, target, i):
        return pltpu.make_async_copy(source, target, loads.at[i])

    fetch = [load(patches, right.at[5], 0)]
    fetch += [load(attend_in.at[:, pl.ds(j * width, width)], attend.at[j], 1 + j) for j in range(3)]
    fetch += [load(project_in, project, 4)]
    fetch += [load(expand_in.at[:, pl.ds(j * width, width)], parts.at[slabs + j], 5 + j) for j in range(slabs)]
    fetch += [load(shrink_in.at[pl.ds(j * width, width)], parts.at[2 * slabs + j], 5 + slabs + j) for j in range(slabs)]
    fetch += [load(cotangent, right.at[0], 5 + 2 * slabs)]
    for copy in fetch:
        copy.start()
    main.greet()

    for i in range(images):
        row = jnp.broadcast_to(tiles[i : i + 1, :].astype(f32), (length, length))
        live = jnp.broadcast_to(valid[i : i + 1, :], (length, length)) == 1
        spot = lax.broadcasted_iota(jnp.int32, (length, length), 0) == lax.broadcasted_iota(
            jnp.int32, (length, length), 1
        )
        bias[i] = jnp.where(((row == row.T) & live) | spot, 0.0, -1000000000.0)
    code_width = signs.shape[1]
    codes[...] = jnp.zeros_like(codes)
    codes[:, :code_width] = ((2 * signs[...] - 1).astype(f32) / math.sqrt(code_width)).astype(bf)
    bottle[...] = jnp.zeros_like(bottle)
    bottle[:, :code_width] = bottle_in[...]
    gain_one[...] = jnp.zeros_like(gain_one)
    gain_two[...] = jnp.zeros_like(gain_two)
    fetch[0].wait()

    @pl.when(encoding)
    def _():
        residual[...] = right[5].astype(f32)

    @pl.when(jnp.logical_not(encoding))
    def _():
        residual[...] = times_transpose(codes[...], bottle[...])

    def norm(gain, normed, factor):
        @over(rows, 64)
        def _(r):
            values = residual[r, :]
            center = values - jnp.mean(values, axis=-1, keepdims=True)
            scale = lax.rsqrt(jnp.mean(center * center, axis=-1, keepdims=True) + 1e-06)
            unscaled = center * scale
            normed[r, :] = unscaled
            factor[r, :] = scale
            temp[r, :] = (unscaled * gain[...]).astype(bf)

    def keep_transpose(source, target):
        half = 8 * ROWS
        for i in range(width // half):
            turned = source[:, i * half : (i + 1) * half].T
            for j in range(8):
                z, y, core = i * 2 + j // 4, (j // 2) % 2, j % 2
                target[place(z, y, core, depth) * ROWS : (place(z, y, core, depth) + 1) * ROWS, :] = turned[
                    j * ROWS : (j + 1) * ROWS
                ]

    norm(first, normed_one, factor_one)
    for j in range(3):
        fetch[1 + j].wait()

        @over(width, 256)
        def _(c):
            right[6 + j, :, c] = dot(temp[...], attend[j, :, c]).astype(bf)

    keep_transpose(temp, left.at[slabs + 2])

    def pair_of(turn):
        image, pair = turn // pairs, turn % pairs
        r = pl.ds(pl.multiple_of(image * length, length), length)
        c = pl.ds(pl.multiple_of(pair * 128, 128), 128)
        return image, r, c

    def masked(values, low, scale=1.0):
        return jnp.where(low_half if low else jnp.logical_not(low_half), values * scale, 0.0).astype(bf)

    @pl.loop(0, images * pairs)
    def _(turn):
        image, r, c = pair_of(turn)
        query, key, value = right[6, r, c], right[7, r, c], right[8, r, c]
        mixed = []
        for head in range(2):
            scores = times_transpose(masked(query, head == 0, HD**-0.5), key) + bias[image]
            raised = jnp.exp(scores - jnp.max(scores, axis=-1, keepdims=True))
            weights = (raised * (1.0 / jnp.sum(raised, axis=-1, keepdims=True))).astype(bf)
            soft[turn, head * length : (head + 1) * length, :] = weights
            mixed.append(dot(weights, value))
        temp[r, c] = jnp.where(low_half, mixed[0], mixed[1]).astype(bf)

    fetch[4].wait()

    @over(width, 256)
    def _(c):
        residual[:, c] += dot(temp[...], project[:, c])

    keep_transpose(temp, left.at[slabs + 1])
    norm(second, normed_two, factor_two)
    keep_transpose(temp, left.at[slabs])

    for j in range(slabs):
        fetch[5 + j].wait()

        @over(width, 256)
        def _(c):
            hidden = dot(temp[...], parts[slabs + j, :, c])
            share = 0.5 + 0.5 * lax.erf(hidden * math.sqrt(0.5))
            slope = share + hidden * jnp.exp(-0.5 * hidden * hidden) * (1.0 / math.sqrt(2.0 * math.pi))
            parts[j, :rows, c] = (hidden * share).astype(bf)
            right[1 + j, :, c] = slope.astype(bf)

    for j in range(slabs):
        fetch[5 + slabs + j].wait()

    @over(width, 256)
    def _(c):
        for j in range(slabs):
            residual[:, c] += dot(parts[j, :rows, :], parts[2 * slabs + j, :, c])

    for i in range(2 * slabs):
        z, y = i // 2, i % 2
        turned = parts[i // 2, :rows, (i % 2) * 8 * ROWS : (i % 2 + 1) * 8 * ROWS].T
        for core in range(2):
            for j in range(slabs):
                spot = place(z, y, core, depth)
                left[j, spot * ROWS : (spot + 1) * ROWS, :] = turned[(core * 4 + j) * ROWS : (core * 4 + j + 1) * ROWS]

    saved[...] = residual[...].astype(bf)
    out_copy = pltpu.make_async_copy(saved, results, loads.at[6 + 2 * slabs])
    across = pltpu.make_async_remote_copy(
        delta, code_grad, code_sems.at[0], code_sems.at[1], device_id=main.peers()[4], device_id_type=MESH
    )
    fetch[5 + 2 * slabs].wait()

    @pl.when(encoding)
    def _():
        latent = dot(saved[...], bottle[...])
        scale = lax.rsqrt(jnp.sum(latent * latent, axis=-1, keepdims=True) + 1e-06)
        unit_code = latent * scale
        across.wait_recv()
        grad_unit = code_grad[...].astype(f32)
        grad_latent = (
            scale * (grad_unit - unit_code * jnp.sum(unit_code * grad_unit, axis=-1, keepdims=True))
        ).astype(bf)
        grad_out = times_transpose(grad_latent, bottle[...])
        residual[...] = grad_out
        right[0] = grad_out.astype(bf)
        bottle_sum[...] = contract_rows(saved[...], grad_latent)

    @pl.when(jnp.logical_not(encoding))
    def _():
        out_copy.start()
        residual[...] = right[0].astype(f32)

    def piece(k):
        a = jnp.minimum(k, slabs) + (k >= 2 * slabs).astype(jnp.int32) + (k > 2 * slabs).astype(jnp.int32)
        b = jnp.maximum(k - slabs + 1, 0)

        @over(width, 256)
        def _(c):
            parts[k, :, c] = dot(left[a], right[b, :, c]).astype(bf)

        main.start(k)

    def norm_back(gain, normed, factor, gain_sum):
        @over(rows, 64)
        def _(r):
            given, unscaled = work[r, :], normed[r, :]
            gain_sum[...] += jnp.sum((given * unscaled).reshape(8, 8, width), axis=0)
            grad = given * gain[...]
            inner = jnp.mean(grad * unscaled, axis=-1, keepdims=True)
            grad = residual[r, :] + factor[r, :] * (grad - jnp.mean(grad, axis=-1, keepdims=True) - unscaled * inner)
            residual[r, :] = grad
            saved[r, :] = grad.astype(bf)

    def chain():
        for j in range(slabs):

            @over(width, 256)
            def _(c):
                grad = times_transpose(right[0], parts[2 * slabs + j, c, :])
                right[1 + j, :, c] = (grad * right[1 + j, :, c].astype(f32)).astype(bf)

        @over(width, 256)
        def _(c):
            grad = times_transpose(right[1], parts[slabs, c, :])
            for j in range(1, slabs):
                grad += times_transpose(right[1 + j], parts[slabs + j, c, :])
            work[:, c] = grad

        @pl.when(jnp.logical_not(encoding))
        def _():
            out_copy.wait()

        norm_back(second, normed_two, factor_two, gain_two)
        right[5] = saved[...]

        @over(width, 256)
        def _(c):
            temp[:, c] = times_transpose(right[5], project[c, :]).astype(bf)

        @pl.loop(0, images * pairs)
        def _(turn):
            image, r, c = pair_of(turn)
            query, key, value, grad = right[6, r, c], right[7, r, c], right[8, r, c], temp[r, c]
            to_query, to_key, to_value = [], [], []
            for head in range(2):
                weights = soft[turn, head * length : (head + 1) * length, :]
                grad_head = masked(grad, head == 0)
                grad_soft = times_transpose(grad_head, value)
                exact = weights.astype(f32)
                inner = jnp.sum(exact * grad_soft, axis=-1, keepdims=True)
                grad_scores = (exact * (grad_soft - inner)).astype(bf)
                to_query.append(dot(grad_scores, key))
                to_key.append(contract_rows(grad_scores, masked(query, head == 0, HD**-0.5)))
                to_value.append(contract_rows(weights, grad_head))
            right[6, r, c] = (jnp.where(low_half, to_query[0], to_query[1]) * HD**-0.5).astype(bf)
            right[7, r, c] = (to_key[0] + to_key[1]).astype(bf)
            right[8, r, c] = (to_value[0] + to_value[1]).astype(bf)

        @over(width, 256)
        def _(c):
            grad = times_transpose(right[6], attend[0, c, :])
            for j in range(1, 3):
                grad += times_transpose(right[6 + j], attend[j, c, :])
            work[:, c] = grad

        norm_back(first, normed_one, factor_one, gain_one)

        @pl.when(jnp.logical_not(encoding))
        def _():
            delta[...] = dot(saved[...], bottle[...]).astype(bf)
            across.start()
            bottle_sum[...] = contract_rows(saved[...], codes[...])

        @pl.when(encoding)
        def _():
            out_copy.start()

    def first_pieces():
        @pl.loop(0, slabs)
        def _(k):
            piece(k)
            at(k - 1, slabs, main.after_core)

    @pl.loop(0, 2)
    def _(phase):
        pl.when(phase == main.section)(first_pieces)
        pl.when(phase != main.section)(chain)

    spare = lax.broadcasted_iota(jnp.int32, (width, 128), 1)
    column_one = jnp.sum(gain_one[...].T, axis=1, keepdims=True)
    column_two = jnp.sum(gain_two[...].T, axis=1, keepdims=True)
    gathered = jnp.where(
        spare == code_width, column_one, jnp.where(spare == code_width + 1, column_two, bottle_sum[...])
    ).astype(bf)
    for i in range(4 * depth):
        spot = place(i // 4, (i // 2) % 2, i % 2, depth)
        extra[0, spot * ROWS : (spot + 1) * ROWS, :] = gathered[i * ROWS : (i + 1) * ROWS]
    small.start(0)

    @pl.loop(slabs, count + depth + slabs)
    def _(t):
        at(t, count, piece)
        at(t - 1, count, main.after_core)
        at(t - slabs - 1, 1, small.after_core)
        main.along(t - slabs, count)
        small.along(t - slabs - 2, 1)

    @pl.when(encoding)
    def _():
        out_copy.wait()

    @pl.when(jnp.logical_not(encoding))
    def _():
        across.wait_send()

    small.drain(0)

    @pl.loop(0, count)
    def _(k):
        main.drain(k)


def train(depth, images, arrays):
    patches, signs, _, _, _, attend, project, expand, shrink, _, _, bottle = arrays
    rows, width = patches.shape
    slabs = shrink.shape[0] // width
    count = 2 * slabs + 4
    pairs, length = width // 128, rows // images
    hbm, vmem = pl.BlockSpec(memory_space=pl.ANY), pl.BlockSpec(memory_space=pltpu.VMEM)
    low, full = lambda *shape: pltpu.VMEM(shape, jnp.bfloat16), lambda *shape: pltpu.VMEM(shape, jnp.float32)
    return pl.pallas_call(
        functools.partial(train_kernel, depth, images),
        out_shape=(
            jax.ShapeDtypeStruct((rows, width), jnp.bfloat16),
            jax.ShapeDtypeStruct((count, ROWS, width), jnp.float32),
            jax.ShapeDtypeStruct((1, ROWS, 128), jnp.float32),
        ),
        in_specs=[hbm, vmem, vmem, vmem, hbm, hbm, hbm, hbm, hbm, vmem, vmem, vmem],
        out_specs=[hbm, vmem, vmem],
        scratch_shapes=[
            low(count, width, width),
            low(3, width, width),
            low(width, width),
            low(slabs + 3, width, rows),
            low(slabs + 5, rows, width),
            low(images * pairs, 2 * length, length),
            low(rows, width),
            low(rows, width),
            full(rows, width),
            full(rows, width),
            full(rows, width),
            full(rows, width),
            full(rows, 1),
            full(rows, 1),
            full(images, length, length),
            low(rows, 128),
            low(width, 128),
            low(rows, 128),
            low(rows, 128),
            full(width, 128),
            full(8, width),
            full(8, width),
            low(1, width, 128),
            pltpu.SemaphoreType.DMA((7 + 2 * slabs,)),
            pltpu.SemaphoreType.DMA((2,)),
        ]
        + Reduction.scratch(depth, count, width)
        + Reduction.scratch(depth, 1, 128),
        compiler_params=pltpu.CompilerParams(collective_id=0, has_side_effects=True, vmem_limit_bytes=63 << 20),
        name="train",
    )(*arrays)


def small_slice(*arrays):
    images = arrays[2].shape[0]
    arrays = arrays[:5] + tuple(member[0] for member in arrays[5:9]) + arrays[9:11] + (arrays[11][0],)
    results, total, rest = train(lax.axis_size("batch") // 4, images, arrays)
    width, code = arrays[11].shape
    slabs = arrays[8].shape[0] // width
    beside = lambda low, high: total[low:high].transpose(1, 0, 2).reshape(ROWS, -1)
    outs = (
        results,
        beside(2 * slabs + 1, total.shape[0]),
        total[2 * slabs],
        beside(slabs, 2 * slabs),
        total[:slabs].reshape(-1, width),
        rest[0, :, code],
        rest[0, :, code + 1],
        rest[0, :, :code],
    )
    return tuple(member[None] for member in outs)


def pick_index(stacked, chosen):
    return lax.dynamic_index_in_dim(stacked, chosen, 0, keepdims=False)


def body(
    patches,
    code_signs,
    tile_ids,
    patch_valid,
    cotangent,
    attend_weight,
    project_weight,
    expand_weight,
    shrink_weight,
    norm_first,
    norm_second,
    bottleneck,
):
    micro_count = tile_ids.shape[0]
    length = tile_ids.shape[1]
    code_width = code_signs.shape[1]
    encoding = lax.axis_index("section") == 0
    encoding_int = encoding.astype(jnp.int32)
    weights = (
        attend_weight[0],
        project_weight[0],
        expand_weight[0],
        shrink_weight[0],
        norm_first[0],
        norm_second[0],
    )
    bottle = bottleneck[0]
    code_values = ((2 * code_signs - 1).astype(jnp.float32) / math.sqrt(code_width)).astype(
        jnp.bfloat16
    )
    block_inputs = []
    outputs_low = []
    unit_codes = []
    unit_factors = []
    decoded_list = []
    kept_list = []
    for turn_index in range(micro_count):
        image_rows = patches[turn_index * length : (turn_index + 1) * length].astype(jnp.float32)
        decoder_in = times_transpose(
            code_values[turn_index * length : (turn_index + 1) * length], bottle
        )
        block_in = jnp.where(encoding, image_rows, decoder_in)
        allowed_keys = allowed(tile_ids[turn_index], patch_valid[turn_index])
        output, kept_parts = block_forward(block_in, weights, allowed_keys)
        output_low = output.astype(jnp.bfloat16)
        latent = jnp.dot(output_low, bottle, preferred_element_type=jnp.float32)
        factor = lax.rsqrt(jnp.sum(latent * latent, axis=-1, keepdims=True) + 1e-06)
        block_inputs.append(block_in)
        outputs_low.append(output_low)
        unit_codes.append(latent * factor)
        unit_factors.append(factor)
        decoded_list.append(output_low)
        kept_list.append(kept_parts)
    block_inputs = jnp.stack(block_inputs)
    outputs_low = jnp.stack(outputs_low)
    unit_codes = jnp.stack(unit_codes)
    unit_factors = jnp.stack(unit_factors)
    kept_stack = jax.tree.map(lambda *members: jnp.stack(members), *kept_list)
    totals = None
    sent_grad = jnp.zeros((length, code_width), jnp.bfloat16)
    input_grads = []
    for turn_index in range(micro_count + 1):
        if turn_index > 0:
            received = passed_along(sent_grad, "section", -1)
        else:
            received = jnp.zeros_like(sent_grad)
        chosen = jnp.clip(turn_index - encoding_int, 0, micro_count - 1)
        turn_flag = jnp.where(encoding, turn_index >= 1, turn_index < micro_count).astype(
            jnp.float32
        )
        kept_parts = jax.tree.map(lambda stacked: pick_index(stacked, chosen), kept_stack)
        unit_code = pick_index(unit_codes, chosen)
        factor = pick_index(unit_factors, chosen)
        output_low = pick_index(outputs_low, chosen)
        grad_unit = received.astype(jnp.float32)
        grad_latent = (
            factor
            * (grad_unit - unit_code * jnp.sum(unit_code * grad_unit, axis=-1, keepdims=True))
        ).astype(jnp.bfloat16)
        grad_encoded = times_transpose(grad_latent, bottle)
        bottle_encoder = contract_rows(output_low, grad_latent)
        given_grad = lax.dynamic_slice_in_dim(cotangent, chosen * length, length, 0).astype(
            jnp.float32
        )
        grad_out = jnp.where(encoding, grad_encoded, given_grad)
        grad_in, grads = block_backward(kept_parts, grad_out, weights)
        grad_in_low = grad_in.astype(jnp.bfloat16)
        code_rows = lax.dynamic_slice_in_dim(code_values, chosen * length, length, 0)
        bottle_decoder = contract_rows(grad_in_low, code_rows)
        sent_grad = jnp.dot(grad_in_low, bottle, preferred_element_type=jnp.float32).astype(
            jnp.bfloat16
        )
        grads = grads + (jnp.where(encoding, bottle_encoder, bottle_decoder),)
        grads = tuple((turn_flag * member for member in grads))
        if turn_index > 0:
            input_grads.append(grad_in_low)
        totals = (
            grads
            if totals is None
            else tuple((former + latter for former, latter in zip(totals, grads)))
        )
    totals = lax.psum_scatter(totals, "batch", scatter_dimension=0, tiled=True)
    pieces = [
        jnp.where(encoding, input_grads[turn_index], decoded_list[turn_index])
        for turn_index in range(micro_count)
    ]
    results = jnp.concatenate(pieces, axis=0)[None]
    return (
        results,
        totals[0][None],
        totals[1][None],
        totals[2][None],
        totals[3][None],
        totals[4][None],
        totals[5][None],
        totals[6][None],
    )


def solution(mesh):
    batch = mesh.shape["batch"]
    return jax.shard_map(
        small_slice if batch == 16 else body,
        mesh=mesh,
        in_specs=(
            P("batch", None),
            P("batch", None),
            P("batch", None),
            P("batch", None),
            P("batch", None),
            P("section", None, None),
            P("section", None, None),
            P("section", None, None),
            P("section", None, None),
            P("section", None),
            P("section", None),
            P("section", None, None),
        ),
        out_specs=(
            P("section", "batch", None),
            P("section", "batch", None),
            P("section", "batch", None),
            P("section", "batch", None),
            P("section", "batch", None),
            P("section", "batch"),
            P("section", "batch"),
            P("section", "batch", None),
        ),
        check_vma=False,
    )
```

profile of v0, /device:TPU:0, one launch (start us, length us, event | category | flops | bytes accessed | tf_op | source)
XLA Modules:
  0.0 190.1 jit_solution(8667877308480775664)
XLA Ops:
  0.6 1.6 copy.23
  2.2 1.6 copy.24.signs
  3.9 174.8 %train.1 = (bf16[512,768]{1,0:T(8,128)(2,1)}, f32[12,48,768]{2,1,0:T(8,128)}, f32[1,48,128]{2,1,0:T(8,128)}) custom-call(bf16[512,768]{1,0:T(8,128)(2,1)} %patches.1, s32[512,18]{1,0:T(8,128)} %copy.24.signs, s32[2,256]{1,0:T(2,128)} %tiles.1, s32[2,256]{1,0:T(2,128)} %valid.1, bf16[512,768]{1,0:T(8,128)(2,1)} %cotangent.1, bf16[768,2304]{1,0:T(8,128)(2,1)} %bitcast.16, ...), custom_call_target="tpu_custom_call" | custom-call | tf_op jit(solution)/shard_map/train/pallas_call | solution.py:697
  178.7 1.5 slice_reduce_fusion
  180.2 1.4 copy.27
  181.6 1.6 slice.22
  183.2 1.0 slice_bitcast_fusion.1
  184.2 2.1 %fusion = (f32[4,48,768]{2,1,0:T(8,128)}, f32[48,4,768]{2,0,1:T(8,128)S(1)}) fusion(f32[12,48,768]{2,1,0:T(8,128)} %get-tuple-element.12), kind=kLoop, calls=%fused_computation.4 | loop fusion | bytes 2359296 | tf_op jit(solution)/shard_map/slice | solution.py:752
  186.4 0.3 copy.25
  186.7 0.0 copy-start
  186.7 1.1 broadcast_in_dim_reshape.9
  187.8 0.4 copy.26
  188.1 1.1 broadcast_in_dim_reshape.10
  189.3 0.0 copy-done
  189.3 0.9 copy.29
Async XLA Ops:
  186.7 2.6 %copy-start = (bf16[512,768]{1,0:T(8,128)(2,1)S(1)}, bf16[512,768]{1,0:T(8,128)(2,1)}, u32[]{:S(2)}) copy-start(bf16[512,768]{1,0:T(8,128)(2,1)} %get-tuple-element.11) | copy-start | bytes 2359300
where the time goes:
time: 191 us; the launch traced here: 190 us
  Pallas kernels  175 us (92%)
  local copies, waits for them, and re-layouts  14.7 us (8%)
    pallas_call x1, Pallas kernels, train(): pl.pallas_call(functools.partial(train_kernel, depth, images), out_shape=...  175 us
    unnamed x6, local copies, waits for them, and re-layouts  5.54 us

commit v1 on v0

--- a/solution.py
+++ b/solution.py
@@ -12,6 +12,7 @@
 HD = 64
 MESH = pl.DeviceIdType.MESH
 ROWS = 48
+SLOTS = 8
 
 
 def passed_along(block, axis, distance):
@@ -179,18 +180,19 @@
         self.parts, self.total = parts, total
         self.from_core, self.from_y, self.from_low, self.from_high = scratch[:4]
         self.core_s, self.core_r, self.y_s, self.y_r = scratch[4:8]
-        self.up_s, self.up_r, self.down_s, self.down_r = scratch[8:12]
+        self.up_s, self.up_r, self.down_s, self.down_r, self.free = scratch[8:13]
         self.section = lax.axis_index("section")
         self.me = lax.axis_index("batch")
         self.z, self.y, self.core = self.me // 4, (self.me // 2) % 2, self.me % 2
 
     def scratch(depth, count, wide):
         return (
-            [pltpu.VMEM((count, 2 * depth * ROWS, wide), jnp.bfloat16)]
+            [pltpu.VMEM((min(count, SLOTS), 2 * depth * ROWS, wide), jnp.bfloat16)]
             + [pltpu.VMEM((count, depth * ROWS, wide), jnp.bfloat16)]
             + [pltpu.VMEM((count, (depth - 1) * ROWS, wide), jnp.bfloat16)] * 2
             + [pltpu.SemaphoreType.DMA((count,))] * 4
             + [pltpu.SemaphoreType.DMA((count, depth))] * 4
+            + [pltpu.SemaphoreType.REGULAR]
         )
 
     def peers(self):
@@ -241,7 +243,7 @@
         half = 2 * self.depth * ROWS
         return pltpu.make_async_remote_copy(
             self.parts.at[k, pl.ds(pl.multiple_of((1 - self.core) * half, half), half)],
-            self.from_core.at[k], self.core_s.at[k], self.core_r.at[k],
+            self.from_core.at[k % SLOTS], self.core_s.at[k], self.core_r.at[k],
             device_id=self.peers()[0], device_id_type=MESH,
         )
 
@@ -272,6 +274,10 @@
         here[...] = (here[...].astype(jnp.float32) + other.astype(jnp.float32)).astype(jnp.bfloat16)
 
     def start(self, k):
+        @pl.when(k >= SLOTS)
+        def _():
+            pl.semaphore_wait(self.free, 1)
+
         self.core_copy(k).start()
 
     def after_core(self, k):
@@ -281,10 +287,14 @@
 
             @pl.loop(0, self.depth)
             def _(to):
-                self.add(self.block(k, self.core, half, to), self.from_core[k, rows_of(half * self.depth + to)])
+                self.add(self.block(k, self.core, half, to), self.from_core[k % SLOTS, rows_of(half * self.depth + to)])
 
             if far:
                 self.y_copy(k).start()
+
+        @pl.when(k + SLOTS < self.parts.shape[0])
+        def _():
+            pl.semaphore_signal(self.free, inc=1, device_id=self.peers()[0], device_id_type=MESH)
 
     def after_y(self, k):
         self.y_copy(k).wait_recv()
@@ -329,18 +339,18 @@
         @pl.when(self.z == 0)
         def _():
             self.down_copy(k, self.z).wait_recv()
-            self.total[k] = own[...].astype(jnp.float32) + high[...].astype(jnp.float32)
+            self.total[rows_of(k), :] = own[...].astype(jnp.float32) + high[...].astype(jnp.float32)
 
         @pl.when(self.z == self.depth - 1)
         def _():
             self.up_copy(k, self.z).wait_recv()
-            self.total[k] = own[...].astype(jnp.float32) + low[...].astype(jnp.float32)
+            self.total[rows_of(k), :] = own[...].astype(jnp.float32) + low[...].astype(jnp.float32)
 
         @pl.when((self.z > 0) & (self.z < self.depth - 1))
         def _():
             self.down_copy(k, self.z).wait_recv()
             self.up_copy(k, self.z).wait_recv()
-            self.total[k] = (
+            self.total[rows_of(k), :] = (
                 own[...].astype(jnp.float32) + high[...].astype(jnp.float32) + low[...].astype(jnp.float32)
             )
 
@@ -384,16 +394,17 @@
     depth, images,
     patches, signs, tiles, valid, cotangent, attend_in, project_in, expand_in, shrink_in, first, second, bottle_in,
     results, total, rest,
-    parts, attend, project, left, right, soft, temp, saved, normed_one, normed_two, residual, work, factor_one,
+    parts, attend, project, left, right, soft, temp, saved, normed_one, normed_two, residual, factor_one,
     factor_two, bias, codes, bottle, delta, code_grad, bottle_sum, gain_one, gain_two, extra,
     loads, code_sems, *scratch,
 ):
     rows, width = patches.shape
     length = rows // images
+    work = total.at[:rows]
     count, slabs = parts.shape[0], shrink_in.shape[0] // width
     pairs = width // 128
-    main = Reduction(depth, parts, total, scratch[:12])
-    small = Reduction(depth, extra, rest, scratch[12:24])
+    main = Reduction(depth, parts, total, scratch[:13])
+    small = Reduction(depth, extra, rest, scratch[13:26])
     encoding = main.section == 0
     lane = lax.broadcasted_iota(jnp.int32, (length, 128), 1)
     low_half = lane < HD
@@ -422,11 +433,12 @@
             jnp.int32, (length, length), 1
         )
         bias[i] = jnp.where(((row == row.T) & live) | spot, 0.0, -1000000000.0)
-    code_width = signs.shape[1]
-    codes[...] = jnp.zeros_like(codes)
-    codes[:, :code_width] = ((2 * signs[...] - 1).astype(f32) / math.sqrt(code_width)).astype(bf)
-    bottle[...] = jnp.zeros_like(bottle)
-    bottle[:, :code_width] = bottle_in[...]
+    code_width = signs.shape[0]
+    work[:256, :] = jnp.zeros((256, width), f32)
+    work[:code_width, :rows] = (2 * signs[...] - 1).astype(f32) / math.sqrt(code_width)
+    work[128 : 128 + code_width, :] = bottle_in[...].astype(f32)
+    codes[...] = work[:128, :rows].T.astype(bf)
+    bottle[...] = work[128:256, :].T.astype(bf)
     gain_one[...] = jnp.zeros_like(gain_one)
     gain_two[...] = jnp.zeros_like(gain_two)
     fetch[0].wait()
@@ -440,15 +452,13 @@
         residual[...] = times_transpose(codes[...], bottle[...])
 
     def norm(gain, normed, factor):
-        @over(rows, 64)
-        def _(r):
-            values = residual[r, :]
-            center = values - jnp.mean(values, axis=-1, keepdims=True)
-            scale = lax.rsqrt(jnp.mean(center * center, axis=-1, keepdims=True) + 1e-06)
-            unscaled = center * scale
-            normed[r, :] = unscaled
-            factor[r, :] = scale
-            temp[r, :] = (unscaled * gain[...]).astype(bf)
+        values = residual[...]
+        center = values - jnp.mean(values, axis=-1, keepdims=True)
+        scale = lax.rsqrt(jnp.mean(center * center, axis=-1, keepdims=True) + 1e-06)
+        unscaled = center * scale
+        normed[...] = unscaled
+        factor[...] = scale
+        temp[...] = (unscaled * gain[...]).astype(bf)
 
     def keep_transpose(source, target):
         half = 8 * ROWS
@@ -463,40 +473,43 @@
     norm(first, normed_one, factor_one)
     for j in range(3):
         fetch[1 + j].wait()
-
-        @over(width, 256)
-        def _(c):
-            right[6 + j, :, c] = dot(temp[...], attend[j, :, c]).astype(bf)
+        right[6 + j] = dot(temp[...], attend[j]).astype(bf)
 
     keep_transpose(temp, left.at[slabs + 2])
 
-    def pair_of(turn):
-        image, pair = turn // pairs, turn % pairs
-        r = pl.ds(pl.multiple_of(image * length, length), length)
-        c = pl.ds(pl.multiple_of(pair * 128, 128), 128)
-        return image, r, c
+    group = 3
+    heads = [(pair, head) for pair in range(group) for head in range(2)]
+
+    def group_of(turn):
+        image = turn * group // pairs
+        start = turn * group - image * pairs
+        lanes = [pl.ds(pl.multiple_of((start + pair) * 128, 128), 128) for pair in range(group)]
+        return pl.ds(pl.multiple_of(image * length, length), length), lanes, image
 
     def masked(values, low, scale=1.0):
         return jnp.where(low_half if low else jnp.logical_not(low_half), values * scale, 0.0).astype(bf)
 
-    @pl.loop(0, images * pairs)
+    def merged(members, pair):
+        return jnp.where(low_half, members[2 * pair], members[2 * pair + 1])
+
+    @pl.loop(0, images * pairs // group)
     def _(turn):
-        image, r, c = pair_of(turn)
-        query, key, value = right[6, r, c], right[7, r, c], right[8, r, c]
-        mixed = []
-        for head in range(2):
-            scores = times_transpose(masked(query, head == 0, HD**-0.5), key) + bias[image]
-            raised = jnp.exp(scores - jnp.max(scores, axis=-1, keepdims=True))
-            weights = (raised * (1.0 / jnp.sum(raised, axis=-1, keepdims=True))).astype(bf)
-            soft[turn, head * length : (head + 1) * length, :] = weights
-            mixed.append(dot(weights, value))
-        temp[r, c] = jnp.where(low_half, mixed[0], mixed[1]).astype(bf)
+        r, lanes, image = group_of(turn)
+        query, key, value = ([right[6 + j, r, c] for c in lanes] for j in range(3))
+        scores = [
+            times_transpose(masked(query[pair], head == 0, HD**-0.5), key[pair]) + bias[image] for pair, head in heads
+        ]
+        raised = [jnp.exp(member - jnp.max(member, axis=-1, keepdims=True)) for member in scores]
+        weights = [(member * (1.0 / jnp.sum(member, axis=-1, keepdims=True))).astype(bf) for member in raised]
+        for (pair, head), member in zip(heads, weights):
+            soft[turn * group + pair, head * length : (head + 1) * length, :] = member
+        mixed = [dot(member, value[pair]) for (pair, head), member in zip(heads, weights)]
+        for pair, c in enumerate(lanes):
+            temp[r, c] = merged(mixed, pair).astype(bf)
 
     fetch[4].wait()
 
-    @over(width, 256)
-    def _(c):
-        residual[:, c] += dot(temp[...], project[:, c])
+    residual[...] += dot(temp[...], project[...])
 
     keep_transpose(temp, left.at[slabs + 1])
     norm(second, normed_two, factor_two)
@@ -505,21 +518,15 @@
     for j in range(slabs):
         fetch[5 + j].wait()
 
-        @over(width, 256)
-        def _(c):
-            hidden = dot(temp[...], parts[slabs + j, :, c])
-            share = 0.5 + 0.5 * lax.erf(hidden * math.sqrt(0.5))
-            slope = share + hidden * jnp.exp(-0.5 * hidden * hidden) * (1.0 / math.sqrt(2.0 * math.pi))
-            parts[j, :rows, c] = (hidden * share).astype(bf)
-            right[1 + j, :, c] = slope.astype(bf)
+        hidden = dot(temp[...], parts[slabs + j])
+        share = 0.5 + 0.5 * lax.erf(hidden * math.sqrt(0.5))
+        slope = share + hidden * jnp.exp(-0.5 * hidden * hidden) * (1.0 / math.sqrt(2.0 * math.pi))
+        parts[j, :rows, :] = (hidden * share).astype(bf)
+        right[1 + j] = slope.astype(bf)
 
     for j in range(slabs):
         fetch[5 + slabs + j].wait()
-
-    @over(width, 256)
-    def _(c):
-        for j in range(slabs):
-            residual[:, c] += dot(parts[j, :rows, :], parts[2 * slabs + j, :, c])
+        residual[...] += dot(parts[j, :rows, :], parts[2 * slabs + j])
 
     for i in range(2 * slabs):
         z, y = i // 2, i % 2
@@ -560,76 +567,66 @@
         a = jnp.minimum(k, slabs) + (k >= 2 * slabs).astype(jnp.int32) + (k > 2 * slabs).astype(jnp.int32)
         b = jnp.maximum(k - slabs + 1, 0)
 
-        @over(width, 256)
-        def _(c):
-            parts[k, :, c] = dot(left[a], right[b, :, c]).astype(bf)
-
+        parts[k] = dot(left[a], right[b]).astype(bf)
         main.start(k)
 
-    def norm_back(gain, normed, factor, gain_sum):
-        @over(rows, 64)
+    def norm_back(gain, normed, factor, gain_sum, low):
+        @over(rows, length)
         def _(r):
             given, unscaled = work[r, :], normed[r, :]
-            gain_sum[...] += jnp.sum((given * unscaled).reshape(8, 8, width), axis=0)
+            gain_sum[...] += jnp.sum((given * unscaled).reshape(-1, 8, width), axis=0)
             grad = given * gain[...]
             inner = jnp.mean(grad * unscaled, axis=-1, keepdims=True)
             grad = residual[r, :] + factor[r, :] * (grad - jnp.mean(grad, axis=-1, keepdims=True) - unscaled * inner)
             residual[r, :] = grad
-            saved[r, :] = grad.astype(bf)
+            low[r, :] = grad.astype(bf)
 
     def chain():
         for j in range(slabs):
-
-            @over(width, 256)
-            def _(c):
-                grad = times_transpose(right[0], parts[2 * slabs + j, c, :])
-                right[1 + j, :, c] = (grad * right[1 + j, :, c].astype(f32)).astype(bf)
-
-        @over(width, 256)
-        def _(c):
-            grad = times_transpose(right[1], parts[slabs, c, :])
-            for j in range(1, slabs):
-                grad += times_transpose(right[1 + j], parts[slabs + j, c, :])
-            work[:, c] = grad
+            grad = times_transpose(right[0], parts[2 * slabs + j])
+            right[1 + j] = (grad * right[1 + j].astype(f32)).astype(bf)
+        grad = times_transpose(right[1], parts[slabs])
+        for j in range(1, slabs):
+            grad += times_transpose(right[1 + j], parts[slabs + j])
+        work[...] = grad
+
+        norm_back(second, normed_two, factor_two, gain_two, right.at[5])
+
+        temp[...] = times_transpose(right[5], project[...]).astype(bf)
+
+        @pl.loop(0, images * pairs // group)
+        def _(turn):
+            r, lanes, image = group_of(turn)
+            query, key, value = ([right[6 + j, r, c] for c in lanes] for j in range(3))
+            weights = [soft[turn * group + pair, head * length : (head + 1) * length, :] for pair, head in heads]
+            grad_heads = [masked(temp[r, lanes[pair]], head == 0) for pair, head in heads]
+            grad_soft = [times_transpose(member, value[pair]) for (pair, head), member in zip(heads, grad_heads)]
+            grad_scores = []
+            for low, member in zip(weights, grad_soft):
+                exact = low.astype(f32)
+                inner = jnp.sum(exact * member, axis=-1, keepdims=True)
+                grad_scores.append((exact * (member - inner)).astype(bf))
+            to_query = [dot(member, key[pair]) for (pair, head), member in zip(heads, grad_scores)]
+            to_key = [
+                contract_rows(member, masked(query[pair], head == 0, HD**-0.5))
+                for (pair, head), member in zip(heads, grad_scores)
+            ]
+            to_value = [contract_rows(low, member) for low, member in zip(weights, grad_heads)]
+            for pair, c in enumerate(lanes):
+                right[6, r, c] = (merged(to_query, pair) * HD**-0.5).astype(bf)
+                right[7, r, c] = (to_key[2 * pair] + to_key[2 * pair + 1]).astype(bf)
+                right[8, r, c] = (to_value[2 * pair] + to_value[2 * pair + 1]).astype(bf)
+
+        grad = times_transpose(right[6], attend[0])
+        for j in range(1, 3):
+            grad += times_transpose(right[6 + j], attend[j])
+        work[...] = grad
 
         @pl.when(jnp.logical_not(encoding))
         def _():
             out_copy.wait()
 
-        norm_back(second, normed_two, factor_two, gain_two)
-        right[5] = saved[...]
-
-        @over(width, 256)
-        def _(c):
-            temp[:, c] = times_transpose(right[5], project[c, :]).astype(bf)
-
-        @pl.loop(0, images * pairs)
-        def _(turn):
-            image, r, c = pair_of(turn)
-            query, key, value, grad = right[6, r, c], right[7, r, c], right[8, r, c], temp[r, c]
-            to_query, to_key, to_value = [], [], []
-            for head in range(2):
-                weights = soft[turn, head * length : (head + 1) * length, :]
-                grad_head = masked(grad, head == 0)
-                grad_soft = times_transpose(grad_head, value)
-                exact = weights.astype(f32)
-                inner = jnp.sum(exact * grad_soft, axis=-1, keepdims=True)
-                grad_scores = (exact * (grad_soft - inner)).astype(bf)
-                to_query.append(dot(grad_scores, key))
-                to_key.append(contract_rows(grad_scores, masked(query, head == 0, HD**-0.5)))
-                to_value.append(contract_rows(weights, grad_head))
-            right[6, r, c] = (jnp.where(low_half, to_query[0], to_query[1]) * HD**-0.5).astype(bf)
-            right[7, r, c] = (to_key[0] + to_key[1]).astype(bf)
-            right[8, r, c] = (to_value[0] + to_value[1]).astype(bf)
-
-        @over(width, 256)
-        def _(c):
-            grad = times_transpose(right[6], attend[0, c, :])
-            for j in range(1, 3):
-                grad += times_transpose(right[6 + j], attend[j, c, :])
-            work[:, c] = grad
-
-        norm_back(first, normed_one, factor_one, gain_one)
+        norm_back(first, normed_one, factor_one, gain_one, saved)
 
         @pl.when(jnp.logical_not(encoding))
         def _():
@@ -698,8 +695,8 @@
         functools.partial(train_kernel, depth, images),
         out_shape=(
             jax.ShapeDtypeStruct((rows, width), jnp.bfloat16),
-            jax.ShapeDtypeStruct((count, ROWS, width), jnp.float32),
-            jax.ShapeDtypeStruct((1, ROWS, 128), jnp.float32),
+            jax.ShapeDtypeStruct((count * ROWS, width), jnp.float32),
+            jax.ShapeDtypeStruct((ROWS, 128), jnp.float32),
         ),
         in_specs=[hbm, vmem, vmem, vmem, hbm, hbm, hbm, hbm, hbm, vmem, vmem, vmem],
         out_specs=[hbm, vmem, vmem],
@@ -712,7 +709,6 @@
             low(images * pairs, 2 * length, length),
             low(rows, width),
             low(rows, width),
-            full(rows, width),
             full(rows, width),
             full(rows, width),
             full(rows, width),
@@ -737,24 +733,56 @@
     )(*arrays)
 
 
-def small_slice(*arrays):
+def deliver_kernel(slabs, code, raw, total, rest, results, attend, project, expand, shrink, first, second, bottle):
+    width = total.shape[1]
+    results[...] = raw[...]
+    for j in range(slabs):
+        shrink[j * ROWS : (j + 1) * ROWS, :] = total[j * ROWS : (j + 1) * ROWS, :]
+        expand[:, j * width : (j + 1) * width] = total[(slabs + j) * ROWS : (slabs + j + 1) * ROWS, :]
+    project[...] = total[2 * slabs * ROWS : (2 * slabs + 1) * ROWS, :]
+    for j in range(3):
+        start = (2 * slabs + 1 + j) * ROWS
+        attend[:, j * width : (j + 1) * width] = total[start : start + ROWS, :]
+    turned = rest[...].T
+    first[...] = turned[code : code + 1]
+    second[...] = turned[code + 1 : code + 2]
+    for i in range(code):
+        bottle[i] = turned[i : i + 1]
+
+
+def deliver(raw, total, rest, slabs, code):
+    width = total.shape[1]
+    vmem = pl.BlockSpec(memory_space=pltpu.VMEM)
+    full = lambda *shape: jax.ShapeDtypeStruct(shape, jnp.float32)
+    return pl.pallas_call(
+        functools.partial(deliver_kernel, slabs, code),
+        out_shape=(
+            jax.ShapeDtypeStruct(raw.shape, raw.dtype),
+            full(ROWS, 3 * width),
+            full(ROWS, width),
+            full(ROWS, slabs * width),
+            full(slabs * ROWS, width),
+            full(1, ROWS),
+            full(1, ROWS),
+            full(code, 1, ROWS),
+        ),
+        in_specs=[vmem] * 3,
+        out_specs=[vmem] * 8,
+        name="deliver",
+    )(raw, total, rest)
+
+
+def two_images(*arrays):
     images = arrays[2].shape[0]
-    arrays = arrays[:5] + tuple(member[0] for member in arrays[5:9]) + arrays[9:11] + (arrays[11][0],)
-    results, total, rest = train(lax.axis_size("batch") // 4, images, arrays)
-    width, code = arrays[11].shape
-    slabs = arrays[8].shape[0] // width
-    beside = lambda low, high: total[low:high].transpose(1, 0, 2).reshape(ROWS, -1)
-    outs = (
-        results,
-        beside(2 * slabs + 1, total.shape[0]),
-        total[2 * slabs],
-        beside(slabs, 2 * slabs),
-        total[:slabs].reshape(-1, width),
-        rest[0, :, code],
-        rest[0, :, code + 1],
-        rest[0, :, :code],
-    )
-    return tuple(member[None] for member in outs)
+    code = arrays[1].shape[1]
+    slabs = arrays[8].shape[1] // arrays[0].shape[1]
+    weights = tuple(member[0] for member in arrays[5:9])
+    arrays = (arrays[0], arrays[1].T) + arrays[2:5] + weights + arrays[9:11] + (arrays[11][0].T,)
+    raw, total, rest = train(lax.axis_size("batch") // 4, images, arrays)
+    results, attend, project, expand, shrink, first, second, bottle = deliver(raw, total, rest, slabs, code)
+    return (
+        results[None], attend[None], project[None], expand[None], shrink[None], first, second, bottle.transpose(1, 2, 0)
+    )
 
 
 def pick_index(stacked, chosen):
@@ -884,7 +912,7 @@
 def solution(mesh):
     batch = mesh.shape["batch"]
     return jax.shard_map(
-        small_slice if batch == 16 else body,
+        two_images if batch == 16 else body,
         mesh=mesh,
         in_specs=(
             P("batch", None),

time: 191 us -> 146 us (0.76)
  Pallas kernels: 175 us -> 145 us
  local copies, waits for them, and re-layouts: 14.7 us -> 0 us
    pallas_call x1, Pallas kernels: 175 us -> 142 us  [train(): pl.pallas_call(functools.partial(train_kernel, depth, images), out_shape=...]
    unnamed x6 -> x0, local copies, waits for them, and re-layouts: 5.54 us -> none
    slice x3 -> x0, local copies, waits for them, and re-layouts: 5.24 us -> none  [the longest x1 2.14 us: small_slice(): total[:slabs].reshape(-1, width)]
    pallas_call x0 -> x1, Pallas kernels: none -> 3.17 us  [deliver(): pl.pallas_call(functools.partial(deliver_kernel, slabs, code), out_shape=...]
    another operation x2 -> x0, local copies, waits for them, and re-layouts: 2.19 us -> none  [small_slice(): return tuple((member[None] for member in outs))]
where the time goes in v1:
time: 146 us
  Pallas kernels  145 us (99%)
    pallas_call x1, Pallas kernels, train(): pl.pallas_call(functools.partial(train_kernel, depth, images), out_shape=...  142 us
    pallas_call x1, Pallas kernels, deliver(): pl.pallas_call(functools.partial(deliver_kernel, slabs, code), out_shape=...  3.17 us

profile of v1, /device:TPU:0, one launch (start us, length us, event | category | flops | bytes accessed | tf_op | source)
XLA Modules:
  0.0 145.8 jit_solution(18169135890343144261)
XLA Ops:
  0.6 142.0 %train.1 = (bf16[512,768]{1,0:T(8,128)(2,1)}, f32[576,768]{1,0:T(8,128)}, f32[48,128]{1,0:T(8,128)}) custom-call(bf16[512,768]{1,0:T(8,128)(2,1)} %patches.1, s32[18,512]{1,0:T(8,128)} %bitcast.18, s32[2,256]{1,0:T(2,128)} %tiles.1, s32[2,256]{1,0:T(2,128)} %valid.1, bf16[512,768]{1,0:T(8,128)(2,1)} %cotangent.1, bf16[768,2304]{1,0:T(8,128)(2,1)} %bitcast.16, ...), custom_call_target="tpu_custom_call" | custom-call | tf_op jit(solution)/shard_map/train/pallas_call | solution.py:694
  142.7 3.2 %deliver.1 = (bf16[512,768]{1,0:T(8,128)(2,1)}, f32[48,2304]{1,0:T(8,128)}, f32[48,768]{1,0:T(8,128)}, f32[48,3072]{1,0:T(8,128)}, f32[192,768]{1,0:T(8,128)}, /...) custom-call(bf16[512,768]{1,0:T(8,128)(2,1)} %get-tuple-element.19.raw, ...), custom_call_target="tpu_custom_call" | custom-call | tf_op jit(solution)/shard_map/deliver/pallas_call | solution.py:757

commit v2 on v1

--- a/solution.py
+++ b/solution.py
@@ -12,7 +12,8 @@
 HD = 64
 MESH = pl.DeviceIdType.MESH
 ROWS = 48
-SLOTS = 8
+SLOTS = 6
+EARLY = 2
 
 
 def passed_along(block, axis, distance):
@@ -175,8 +176,9 @@
 
 
 class Reduction:
-    def __init__(self, depth, parts, total, scratch):
-        self.depth = depth
+    def __init__(self, depth, early, parts, total, scratch):
+        self.depth, self.early = depth, early
+        self.count, self.passes = parts.shape[0], parts.shape[0] + early
         self.parts, self.total = parts, total
         self.from_core, self.from_y, self.from_low, self.from_high = scratch[:4]
         self.core_s, self.core_r, self.y_s, self.y_r = scratch[4:8]
@@ -185,56 +187,41 @@
         self.me = lax.axis_index("batch")
         self.z, self.y, self.core = self.me // 4, (self.me // 2) % 2, self.me % 2
 
-    def scratch(depth, count, wide):
+    def scratch(depth, early, count, wide):
+        low, dma = lambda *shape: pltpu.VMEM(shape, jnp.bfloat16), pltpu.SemaphoreType.DMA
+        return [
+            low(min(count, SLOTS), 2 * depth * ROWS, wide),
+            low((count - early) * depth * ROWS + early * ROWS, wide),
+            low(count + early, (depth - 1) * ROWS, wide),
+            low(count + early, (depth - 1) * ROWS, wide),
+        ] + [dma((count,))] * 4 + [dma((count + early, depth))] * 4 + [pltpu.SemaphoreType.REGULAR]
+
+    def device(self, z, y, core):
+        return (self.section, z * 4 + y * 2 + core)
+
+    def peers(self):
         return (
-            [pltpu.VMEM((min(count, SLOTS), 2 * depth * ROWS, wide), jnp.bfloat16)]
-            + [pltpu.VMEM((count, depth * ROWS, wide), jnp.bfloat16)]
-            + [pltpu.VMEM((count, (depth - 1) * ROWS, wide), jnp.bfloat16)] * 2
-            + [pltpu.SemaphoreType.DMA((count,))] * 4
-            + [pltpu.SemaphoreType.DMA((count, depth))] * 4
-            + [pltpu.SemaphoreType.REGULAR]
-        )
-
-    def peers(self):
-        def device(z, y, core):
-            return (self.section, z * 4 + y * 2 + core)
-
-        return (
-            device(self.z, self.y, 1 - self.core),
-            device(self.z, 1 - self.y, self.core),
-            device(jnp.minimum(self.z + 1, self.depth - 1), self.y, self.core),
-            device(jnp.maximum(self.z - 1, 0), self.y, self.core),
+            self.device(self.z, self.y, 1 - self.core),
+            self.device(self.z, 1 - self.y, self.core),
+            self.device(jnp.minimum(self.z + 1, self.depth - 1), self.y, self.core),
+            self.device(jnp.maximum(self.z - 1, 0), self.y, self.core),
             (1 - self.section, self.me),
         )
 
     def greet(self):
         barrier = pltpu.get_barrier_semaphore()
-        core, other, high, low, across = self.peers()
 
         def signal(device):
             pl.semaphore_signal(barrier, inc=1, device_id=device, device_id_type=MESH)
 
-        signal(core)
-        signal(other)
-        signal(across)
-
-        @pl.when(self.z < self.depth - 1)
-        def _():
-            signal(high)
-
-        @pl.when(self.z > 0)
-        def _():
-            signal(low)
-
-        ends = (self.z == 0) | (self.z == self.depth - 1)
-
-        @pl.when(ends)
-        def _():
-            pl.semaphore_wait(barrier, 4)
-
-        @pl.when(jnp.logical_not(ends))
-        def _():
-            pl.semaphore_wait(barrier, 5)
+        core, other, _, _, across = self.peers()
+        for peer in (core, other, across):
+            signal(peer)
+        for z in range(self.depth):
+            pl.when(self.z != z)(lambda z=z: signal(self.device(z, self.y, self.core)))
+
+    def meet(self):
+        pl.semaphore_wait(pltpu.get_barrier_semaphore(), self.depth + 2)
 
     def block(self, k, core, y, z):
         return self.parts.at[k, rows_of(place(z, y, core, self.depth))]
@@ -247,26 +234,53 @@
             device_id=self.peers()[0], device_id_type=MESH,
         )
 
+    def slot(self, k):
+        return jnp.maximum(k - self.early, 0)
+
+    def is_early(self, k):
+        return (k >= 1) & (k <= self.early)
+
     def y_copy(self, k):
         quarter = self.depth * ROWS
-        start = (self.core * 2 + 1 - self.y) * quarter
+        start, slot = (self.core * 2 + 1 - self.y) * quarter, self.slot(k) * quarter
         return pltpu.make_async_remote_copy(
             self.parts.at[k, pl.ds(pl.multiple_of(start, quarter), quarter)],
-            self.from_y.at[k], self.y_s.at[k], self.y_r.at[k],
+            self.from_y.at[pl.ds(pl.multiple_of(slot, quarter), quarter)], self.y_s.at[k], self.y_r.at[k],
             device_id=self.peers()[1], device_id_type=MESH,
         )
 
-    def up_copy(self, k, to):
+    def last_rows(self, k):
+        return rows_of((self.count - self.early) * self.depth + k - 1)
+
+    def last_copy(self, k):
         return pltpu.make_async_remote_copy(
-            self.block(k, self.core, self.y, to), self.from_low.at[k, rows_of(to - 1)],
-            self.up_s.at[k, to], self.up_r.at[k, to],
+            self.block(k, self.core, 1 - self.y, self.z), self.from_y.at[self.last_rows(k)],
+            self.y_s.at[k], self.y_r.at[k],
+            device_id=self.peers()[1], device_id_type=MESH,
+        )
+
+    def of_pass(self, p):
+        if not self.early:
+            return p, self.y
+        soon = p < 2 * self.early
+        piece = jnp.where(soon, 1 + p // 2, jnp.where(p == 2 * self.early, 0, p - self.early))
+        return piece, jnp.where(soon & (p % 2 == 0), 1 - self.y, self.y)
+
+    def pass_block(self, p, to):
+        k, y = self.of_pass(p)
+        return self.block(k, self.core, y, to)
+
+    def up_copy(self, p, to):
+        return pltpu.make_async_remote_copy(
+            self.pass_block(p, to), self.from_low.at[p, rows_of(to - 1)],
+            self.up_s.at[p, to], self.up_r.at[p, to],
             device_id=self.peers()[2], device_id_type=MESH,
         )
 
-    def down_copy(self, k, to):
+    def down_copy(self, p, to):
         return pltpu.make_async_remote_copy(
-            self.block(k, self.core, self.y, to), self.from_high.at[k, rows_of(to)],
-            self.down_s.at[k, to], self.down_r.at[k, to],
+            self.pass_block(p, to), self.from_high.at[p, rows_of(to)],
+            self.down_s.at[p, to], self.down_r.at[p, to],
             device_id=self.peers()[3], device_id_type=MESH,
         )
 
@@ -290,93 +304,143 @@
                 self.add(self.block(k, self.core, half, to), self.from_core[k % SLOTS, rows_of(half * self.depth + to)])
 
             if far:
-                self.y_copy(k).start()
-
-        @pl.when(k + SLOTS < self.parts.shape[0])
+
+                @pl.when(jnp.logical_not(self.is_early(k)))
+                def _():
+                    self.y_copy(k).start()
+
+        @pl.when(k + SLOTS < self.count)
         def _():
             pl.semaphore_signal(self.free, inc=1, device_id=self.peers()[0], device_id_type=MESH)
 
-    def after_y(self, k):
+    def after_y(self, p):
+        k, _ = self.of_pass(p)
         self.y_copy(k).wait_recv()
 
         @pl.loop(0, self.depth)
         def _(to):
-            self.add(self.block(k, self.core, self.y, to), self.from_y[k, rows_of(to)])
-
-    def go_up(self, k):
+            self.add(self.block(k, self.core, self.y, to), self.from_y[rows_of(self.slot(k) * self.depth + to)])
+
+    def go_up(self, p):
         for to in range(self.depth - 1, 0, -1):
 
             @pl.when(self.z < to)
             def _():
-                copy = self.up_copy(k, to)
+                copy = self.up_copy(p, to)
 
                 @pl.when(self.z > 0)
                 def _():
                     copy.wait_recv()
-                    self.add(self.block(k, self.core, self.y, to), self.from_low[k, rows_of(to - 1)])
+                    self.add(self.pass_block(p, to), self.from_low[p, rows_of(to - 1)])
 
                 copy.start()
 
-    def go_down(self, k):
+    def go_down(self, p):
         for to in range(self.depth - 1):
 
             @pl.when(self.z > to)
             def _():
-                copy = self.down_copy(k, to)
+                copy = self.down_copy(p, to)
 
                 @pl.when(self.z < self.depth - 1)
                 def _():
                     copy.wait_recv()
-                    self.add(self.block(k, self.core, self.y, to), self.from_high[k, rows_of(to)])
+                    self.add(self.pass_block(p, to), self.from_high[p, rows_of(to)])
 
                 copy.start()
 
-    def finish(self, k):
-        own = self.block(k, self.core, self.y, self.z)
-        low = self.from_low.at[k, rows_of(jnp.maximum(self.z - 1, 0))]
-        high = self.from_high.at[k, rows_of(jnp.minimum(self.z, self.depth - 2))]
-
-        @pl.when(self.z == 0)
+    def finish(self, p):
+        k, _ = self.of_pass(p)
+        own, total = self.pass_block(p, self.z), self.total.at[rows_of(k)]
+        total[...] = own[...].astype(jnp.float32)
+
+        @pl.when(self.z > 0)
         def _():
-            self.down_copy(k, self.z).wait_recv()
-            self.total[rows_of(k), :] = own[...].astype(jnp.float32) + high[...].astype(jnp.float32)
-
-        @pl.when(self.z == self.depth - 1)
+            self.up_copy(p, self.z).wait_recv()
+            total[...] += self.from_low[p, rows_of(jnp.maximum(self.z - 1, 0))].astype(jnp.float32)
+
+        @pl.when(self.z < self.depth - 1)
         def _():
-            self.up_copy(k, self.z).wait_recv()
-            self.total[rows_of(k), :] = own[...].astype(jnp.float32) + low[...].astype(jnp.float32)
-
-        @pl.when((self.z > 0) & (self.z < self.depth - 1))
-        def _():
-            self.down_copy(k, self.z).wait_recv()
-            self.up_copy(k, self.z).wait_recv()
-            self.total[rows_of(k), :] = (
-                own[...].astype(jnp.float32) + high[...].astype(jnp.float32) + low[...].astype(jnp.float32)
-            )
+            self.down_copy(p, self.z).wait_recv()
+            total[...] += self.from_high[p, rows_of(jnp.minimum(self.z, self.depth - 2))].astype(jnp.float32)
+
+        if self.early:
+
+            @pl.when((p < 2 * self.early) & (p % 2 == 0))
+            def _():
+                own[...] = total[...].astype(jnp.bfloat16)
+                self.last_copy(k).start()
+
+    def after_last(self, k):
+        self.last_copy(k).wait_recv()
+        self.total[rows_of(k), :] += self.from_y[self.last_rows(k)].astype(jnp.float32)
 
     def drain(self, k):
         self.core_copy(k).wait_send()
-        self.y_copy(k).wait_send()
+        if self.early:
+            pl.when(self.is_early(k))(lambda: self.last_copy(k).wait_send())
+        pl.when(jnp.logical_not(self.is_early(k)))(lambda: self.y_copy(k).wait_send())
+
+    def drain_pass(self, p):
         for to in range(self.depth - 1):
 
             @pl.when(self.z < to + 1)
             def _():
-                self.up_copy(k, to + 1).wait_send()
+                self.up_copy(p, to + 1).wait_send()
 
             @pl.when(self.z > to)
             def _():
-                self.down_copy(k, to).wait_send()
-
-    def along(self, t, count):
-        last = self.depth - 1
-        at(t, count, self.after_y)
-        at(t - self.z, count, self.go_up)
-        at(t - last + self.z, count, self.go_down)
-        at(t - 1 - last, count, self.finish)
-
-
-def at(k, count, action):
-    @pl.when((k >= 0) & (k < count))
+                self.down_copy(p, to).wait_send()
+
+    def direct_copy(self, p, to):
+        return pltpu.make_async_remote_copy(
+            self.pass_block(p, to), self.from_low.at[p, rows_of(self.z - (self.z > to).astype(jnp.int32))],
+            self.up_s.at[p, to], self.up_r.at[p, self.z],
+            device_id=self.device(to, self.y, self.core), device_id_type=MESH,
+        )
+
+    def go_direct(self, p):
+        for distance in range(self.depth - 1, 0, -1):
+            pl.when(self.z + distance < self.depth)(lambda: self.direct_copy(p, self.z + distance).start())
+            pl.when(self.z >= distance)(lambda: self.direct_copy(p, self.z - distance).start())
+
+    def finish_direct(self, p):
+        k, _ = self.of_pass(p)
+        total = self.total.at[rows_of(k)]
+        total[...] = self.pass_block(p, self.z)[...].astype(jnp.float32)
+
+        @pl.loop(0, self.depth - 1)
+        def _(i):
+            source = i + (i >= self.z).astype(jnp.int32)
+            arrived = self.from_low.at[p, rows_of(i)]
+            pltpu.make_async_remote_copy(
+                arrived, arrived, self.up_s.at[p, source], self.up_r.at[p, source],
+                device_id=self.device(source, self.y, self.core), device_id_type=MESH,
+            ).wait_recv()
+            total[...] += arrived[...].astype(jnp.float32)
+
+    def drain_direct(self, p):
+        for to in range(self.depth):
+            pl.when(self.z != to)(lambda: self.direct_copy(p, to).wait_send())
+
+    def along(self, t, ahead):
+        last, soon, chained = self.depth - 1, 2 * self.early, self.passes - 1
+        for far, action in ((self.z, self.go_up), (last - self.z, self.go_down)) if chained else ():
+            pl.when(far > 0)(lambda far=far, action=action: at(t - far, 0, chained, action))
+
+        ends = ((self.z == 0, self.go_up), (self.z == last, self.go_down))
+        for end, action in ends:
+            if self.early:
+                pl.when(end)(lambda action=action: at(t + ahead, 0, soon, action))
+        at(t, soon, self.passes, self.after_y)
+        for end, action in ends:
+            if chained:
+                pl.when(end)(lambda action=action: at(t, soon, chained, action))
+        at(t, chained, self.passes, self.go_direct)
+
+
+def at(k, low, high, action):
+    @pl.when((k >= low) & (k < high))
     def _():
         action(k)
 
@@ -395,7 +459,7 @@
     patches, signs, tiles, valid, cotangent, attend_in, project_in, expand_in, shrink_in, first, second, bottle_in,
     results, total, rest,
     parts, attend, project, left, right, soft, temp, saved, normed_one, normed_two, residual, factor_one,
-    factor_two, bias, codes, bottle, delta, code_grad, bottle_sum, gain_one, gain_two, extra,
+    factor_two, average_two, bias, codes, bottle, delta, code_grad, bottle_sum, gain_one, gain_two, extra,
     loads, code_sems, *scratch,
 ):
     rows, width = patches.shape
@@ -403,8 +467,8 @@
     work = total.at[:rows]
     count, slabs = parts.shape[0], shrink_in.shape[0] // width
     pairs = width // 128
-    main = Reduction(depth, parts, total, scratch[:13])
-    small = Reduction(depth, extra, rest, scratch[13:26])
+    main = Reduction(depth, EARLY, parts, total, scratch[:13])
+    small = Reduction(depth, 0, extra, rest, scratch[13:26])
     encoding = main.section == 0
     lane = lax.broadcasted_iota(jnp.int32, (length, 128), 1)
     low_half = lane < HD
@@ -416,15 +480,15 @@
     def load(source, target, i):
         return pltpu.make_async_copy(source, target, loads.at[i])
 
+    main.greet()
     fetch = [load(patches, right.at[5], 0)]
     fetch += [load(attend_in.at[:, pl.ds(j * width, width)], attend.at[j], 1 + j) for j in range(3)]
-    fetch += [load(project_in, project, 4)]
-    fetch += [load(expand_in.at[:, pl.ds(j * width, width)], parts.at[slabs + j], 5 + j) for j in range(slabs)]
-    fetch += [load(shrink_in.at[pl.ds(j * width, width)], parts.at[2 * slabs + j], 5 + slabs + j) for j in range(slabs)]
-    fetch += [load(cotangent, right.at[0], 5 + 2 * slabs)]
     for copy in fetch:
         copy.start()
-    main.greet()
+    fetch += [load(project_in, project, 4)]
+    fetch += [load(expand_in.at[:, pl.ds(j * width, width)], parts.at[2 * slabs + j], 5 + j) for j in range(slabs)]
+    fetch += [load(shrink_in.at[pl.ds(j * width, width)], parts.at[slabs + j], 5 + slabs + j) for j in range(slabs)]
+    fetch += [load(cotangent, right.at[0], 5 + 2 * slabs)]
 
     for i in range(images):
         row = jnp.broadcast_to(tiles[i : i + 1, :].astype(f32), (length, length))
@@ -451,9 +515,12 @@
     def _():
         residual[...] = times_transpose(codes[...], bottle[...])
 
-    def norm(gain, normed, factor):
+    def norm(gain, normed, factor, average=None):
         values = residual[...]
-        center = values - jnp.mean(values, axis=-1, keepdims=True)
+        middle = jnp.mean(values, axis=-1, keepdims=True)
+        if average is not None:
+            average[...] = middle
+        center = values - middle
         scale = lax.rsqrt(jnp.mean(center * center, axis=-1, keepdims=True) + 1e-06)
         unscaled = center * scale
         normed[...] = unscaled
@@ -473,6 +540,9 @@
     norm(first, normed_one, factor_one)
     for j in range(3):
         fetch[1 + j].wait()
+        if j == 2:
+            for copy in fetch[4:]:
+                copy.start()
         right[6 + j] = dot(temp[...], attend[j]).astype(bf)
 
     keep_transpose(temp, left.at[slabs + 2])
@@ -512,56 +582,59 @@
     residual[...] += dot(temp[...], project[...])
 
     keep_transpose(temp, left.at[slabs + 1])
-    norm(second, normed_two, factor_two)
+    norm(second, normed_two, factor_two, average_two)
     keep_transpose(temp, left.at[slabs])
 
     for j in range(slabs):
         fetch[5 + j].wait()
 
-        hidden = dot(temp[...], parts[slabs + j])
+        hidden = dot(temp[...], parts[2 * slabs + j])
         share = 0.5 + 0.5 * lax.erf(hidden * math.sqrt(0.5))
         slope = share + hidden * jnp.exp(-0.5 * hidden * hidden) * (1.0 / math.sqrt(2.0 * math.pi))
         parts[j, :rows, :] = (hidden * share).astype(bf)
         right[1 + j] = slope.astype(bf)
 
-    for j in range(slabs):
-        fetch[5 + slabs + j].wait()
-        residual[...] += dot(parts[j, :rows, :], parts[2 * slabs + j])
-
-    for i in range(2 * slabs):
-        z, y = i // 2, i % 2
-        turned = parts[i // 2, :rows, (i % 2) * 8 * ROWS : (i % 2 + 1) * 8 * ROWS].T
-        for core in range(2):
-            for j in range(slabs):
-                spot = place(z, y, core, depth)
-                left[j, spot * ROWS : (spot + 1) * ROWS, :] = turned[(core * 4 + j) * ROWS : (core * 4 + j + 1) * ROWS]
-
-    saved[...] = residual[...].astype(bf)
+    for copy in fetch[5 + slabs :]:
+        copy.wait()
     out_copy = pltpu.make_async_copy(saved, results, loads.at[6 + 2 * slabs])
     across = pltpu.make_async_remote_copy(
         delta, code_grad, code_sems.at[0], code_sems.at[1], device_id=main.peers()[4], device_id_type=MESH
     )
-    fetch[5 + 2 * slabs].wait()
-
-    @pl.when(encoding)
+    main.meet()
+
+    @pl.when(jnp.logical_not(encoding))
     def _():
+        residual[...] = right[0].astype(f32)
+
+    def block_output():
+        output = normed_two[...] * (1.0 / factor_two[...]) + average_two[...]
+        for j in range(slabs):
+            output += dot(parts[j, :rows, :], parts[slabs + j])
+        saved[...] = output.astype(bf)
+        pl.when(jnp.logical_not(encoding))(out_copy.start)
+        for i in range(2 * slabs):
+            z, y = i // 2, i % 2
+            turned = parts[i // 2, :rows, (i % 2) * 8 * ROWS : (i % 2 + 1) * 8 * ROWS].T
+            for core in range(2):
+                for j in range(slabs):
+                    spot, start = place(z, y, core, depth) * ROWS, (core * 4 + j) * ROWS
+                    left[j, spot : spot + ROWS, :] = turned[start : start + ROWS]
+
+    def from_codes():
         latent = dot(saved[...], bottle[...])
         scale = lax.rsqrt(jnp.sum(latent * latent, axis=-1, keepdims=True) + 1e-06)
         unit_code = latent * scale
+        work[:128, :rows] = jnp.zeros((128, rows), f32)
         across.wait_recv()
-        grad_unit = code_grad[...].astype(f32)
+        work[: delta.shape[0], :rows] = code_grad[...].astype(f32)
+        grad_unit = work[:128, :rows].T
         grad_latent = (
             scale * (grad_unit - unit_code * jnp.sum(unit_code * grad_unit, axis=-1, keepdims=True))
         ).astype(bf)
         grad_out = times_transpose(grad_latent, bottle[...])
+        right[0] = grad_out.astype(bf)
         residual[...] = grad_out
-        right[0] = grad_out.astype(bf)
         bottle_sum[...] = contract_rows(saved[...], grad_latent)
-
-    @pl.when(jnp.logical_not(encoding))
-    def _():
-        out_copy.start()
-        residual[...] = right[0].astype(f32)
 
     def piece(k):
         a = jnp.minimum(k, slabs) + (k >= 2 * slabs).astype(jnp.int32) + (k > 2 * slabs).astype(jnp.int32)
@@ -581,20 +654,24 @@
             residual[r, :] = grad
             low[r, :] = grad.astype(bf)
 
-    def chain():
+    def through_shrink():
         for j in range(slabs):
-            grad = times_transpose(right[0], parts[2 * slabs + j])
+            grad = times_transpose(right[0], parts[slabs + j])
             right[1 + j] = (grad * right[1 + j].astype(f32)).astype(bf)
-        grad = times_transpose(right[1], parts[slabs])
+
+    def through_expand():
+        grad = times_transpose(right[1], parts[2 * slabs])
         for j in range(1, slabs):
-            grad += times_transpose(right[1 + j], parts[slabs + j])
+            grad += times_transpose(right[1 + j], parts[2 * slabs + j])
         work[...] = grad
 
+    def through_project():
         norm_back(second, normed_two, factor_two, gain_two, right.at[5])
 
         temp[...] = times_transpose(right[5], project[...]).astype(bf)
 
-        @pl.loop(0, images * pairs // group)
+    def through_heads(low, high):
+        @pl.loop(low, high)
         def _(turn):
             r, lanes, image = group_of(turn)
             query, key, value = ([right[6 + j, r, c] for c in lanes] for j in range(3))
@@ -617,20 +694,17 @@
                 right[7, r, c] = (to_key[2 * pair] + to_key[2 * pair + 1]).astype(bf)
                 right[8, r, c] = (to_value[2 * pair] + to_value[2 * pair + 1]).astype(bf)
 
+    def through_attend():
         grad = times_transpose(right[6], attend[0])
         for j in range(1, 3):
             grad += times_transpose(right[6 + j], attend[j])
         work[...] = grad
+        norm_back(first, normed_one, factor_one, gain_one, saved)
 
         @pl.when(jnp.logical_not(encoding))
         def _():
-            out_copy.wait()
-
-        norm_back(first, normed_one, factor_one, gain_one, saved)
-
-        @pl.when(jnp.logical_not(encoding))
-        def _():
-            delta[...] = dot(saved[...], bottle[...]).astype(bf)
+            turned = lax.dot_general(bottle[...], saved[...], (((0,), (1,)), ((), ())), preferred_element_type=f32)
+            delta[...] = turned[: delta.shape[0]].astype(bf)
             across.start()
             bottle_sum[...] = contract_rows(saved[...], codes[...])
 
@@ -638,49 +712,58 @@
         def _():
             out_copy.start()
 
-    def first_pieces():
-        @pl.loop(0, slabs)
-        def _(k):
-            piece(k)
-            at(k - 1, slabs, main.after_core)
-
-    @pl.loop(0, 2)
-    def _(phase):
-        pl.when(phase == main.section)(first_pieces)
-        pl.when(phase != main.section)(chain)
-
-    spare = lax.broadcasted_iota(jnp.int32, (width, 128), 1)
-    column_one = jnp.sum(gain_one[...].T, axis=1, keepdims=True)
-    column_two = jnp.sum(gain_two[...].T, axis=1, keepdims=True)
-    gathered = jnp.where(
-        spare == code_width, column_one, jnp.where(spare == code_width + 1, column_two, bottle_sum[...])
-    ).astype(bf)
-    for i in range(4 * depth):
-        spot = place(i // 4, (i // 2) % 2, i % 2, depth)
-        extra[0, spot * ROWS : (spot + 1) * ROWS, :] = gathered[i * ROWS : (i + 1) * ROWS]
-    small.start(0)
-
-    @pl.loop(slabs, count + depth + slabs)
-    def _(t):
-        at(t, count, piece)
-        at(t - 1, count, main.after_core)
-        at(t - slabs - 1, 1, small.after_core)
-        main.along(t - slabs, count)
-        small.along(t - slabs - 2, 1)
-
-    @pl.when(encoding)
-    def _():
-        out_copy.wait()
+        spare = lax.broadcasted_iota(jnp.int32, (width, 128), 1)
+        column_one = jnp.sum(gain_one[...].T, axis=1, keepdims=True)
+        column_two = jnp.sum(gain_two[...].T, axis=1, keepdims=True)
+        gathered = jnp.where(
+            spare == code_width, column_one, jnp.where(spare == code_width + 1, column_two, bottle_sum[...])
+        ).astype(bf)
+        for i in range(4 * depth):
+            spot = place(i // 4, (i // 2) % 2, i % 2, depth)
+            extra[0, spot * ROWS : (spot + 1) * ROWS, :] = gathered[i * ROWS : (i + 1) * ROWS]
+        small.start(0)
+
+    turns = images * pairs // group
+    links, within, last = 6, slabs, depth - 1
+
+    @pl.loop(0, links + main.passes + slabs + 6)
+    def _(step):
+        k = step - links * main.section
+        link = step - within * (1 - main.section)
+        pl.when(k == 0)(block_output)
+        pl.when((k == 0) & encoding)(from_codes)
+        at(k - (k > slabs).astype(jnp.int32), 0, jnp.where(k == slabs, 0, count), piece)
+        at(k - 2, 0, count, main.after_core)
+        at(k - slabs - 6, 0, 1, small.after_core)
+        main.along(k - 5, 2)
+        small.along(k - slabs - 12, 0)
+        at(k - 10, 0, main.passes - 1, main.finish)
+        at(k - 10, main.passes - 1, main.passes, main.finish_direct)
+        at(k - slabs - 16, 0, 1, small.finish_direct)
+        at(k - 15, 1, 1 + EARLY, main.after_last)
+        pl.when(link == 0)(through_shrink)
+        pl.when(link == 1)(through_expand)
+        pl.when(link == 2)(through_project)
+        pl.when((link == 3) | (link == 4))(lambda: through_heads((link - 3) * turns // 2, (link - 2) * turns // 2))
+        pl.when(link == 5)(through_attend)
+
+    out_copy.wait()
 
     @pl.when(jnp.logical_not(encoding))
     def _():
         across.wait_send()
 
     small.drain(0)
+    small.drain_direct(0)
+    main.drain_direct(main.passes - 1)
 
     @pl.loop(0, count)
     def _(k):
         main.drain(k)
+
+    @pl.loop(0, main.passes - 1)
+    def _(p):
+        main.drain_pass(p)
 
 
 def train(depth, images, arrays):
@@ -689,6 +772,7 @@
     slabs = shrink.shape[0] // width
     count = 2 * slabs + 4
     pairs, length = width // 128, rows // images
+    code_rows = -(-signs.shape[0] // 16) * 16
     hbm, vmem = pl.BlockSpec(memory_space=pl.ANY), pl.BlockSpec(memory_space=pltpu.VMEM)
     low, full = lambda *shape: pltpu.VMEM(shape, jnp.bfloat16), lambda *shape: pltpu.VMEM(shape, jnp.float32)
     return pl.pallas_call(
@@ -714,11 +798,12 @@
             full(rows, width),
             full(rows, 1),
             full(rows, 1),
+            full(rows, 1),
             full(images, length, length),
             low(rows, 128),
             low(width, 128),
-            low(rows, 128),
-            low(rows, 128),
+            low(code_rows, rows),
+            low(code_rows, rows),
             full(width, 128),
             full(8, width),
             full(8, width),
@@ -726,8 +811,8 @@
             pltpu.SemaphoreType.DMA((7 + 2 * slabs,)),
             pltpu.SemaphoreType.DMA((2,)),
         ]
-        + Reduction.scratch(depth, count, width)
-        + Reduction.scratch(depth, 1, 128),
+        + Reduction.scratch(depth, EARLY, count, width)
+        + Reduction.scratch(depth, 0, 1, 128),
         compiler_params=pltpu.CompilerParams(collective_id=0, has_side_effects=True, vmem_limit_bytes=63 << 20),
         name="train",
     )(*arrays)

time: 146 us -> 128 us (0.88)
  Pallas kernels: 145 us -> 127 us
    pallas_call x1, Pallas kernels: 142 us -> 124 us  [train(): pl.pallas_call(functools.partial(train_kernel, depth, images), out_shape=...]
where the time goes in v2:
time: 128 us
  Pallas kernels  127 us (99%)
    pallas_call x1, Pallas kernels, train(): pl.pallas_call(functools.partial(train_kernel, depth, images), out_shape=...  124 us
    pallas_call x1, Pallas kernels, deliver(): pl.pallas_call(functools.partial(deliver_kernel, slabs, code), out_shape=...  3.17 us

profile of v2, /device:TPU:0, one launch (start us, length us, event | category | flops | bytes accessed | tf_op | source)
XLA Modules:
  0.0 128.1 jit_solution(4878021333355774992)
XLA Ops:
  0.6 124.2 %train.1 = (bf16[512,768]{1,0:T(8,128)(2,1)}, f32[576,768]{1,0:T(8,128)}, f32[48,128]{1,0:T(8,128)}) custom-call(bf16[512,768]{1,0:T(8,128)(2,1)} %patches.1, s32[18,512]{1,0:T(8,128)} %bitcast.18, s32[2,256]{1,0:T(2,128)} %tiles.1, s32[2,256]{1,0:T(2,128)} %valid.1, bf16[512,768]{1,0:T(8,128)(2,1)} %cotangent.1, bf16[768,2304]{1,0:T(8,128)(2,1)} %bitcast.16, ...), custom_call_target="tpu_custom_call" | custom-call | tf_op jit(solution)/shard_map/train/pallas_call | solution.py:778
  124.9 3.2 %deliver.1 = (bf16[512,768]{1,0:T(8,128)(2,1)}, f32[48,2304]{1,0:T(8,128)}, f32[48,768]{1,0:T(8,128)}, f32[48,3072]{1,0:T(8,128)}, f32[192,768]{1,0:T(8,128)}, /...) custom-call(bf16[512,768]{1,0:T(8,128)(2,1)} %get-tuple-element.19.raw, ...), custom_call_target="tpu_custom_call" | custom-call | tf_op jit(solution)/shard_map/deliver/pallas_call | solution.py:842

commit v3 on v2

--- a/solution.py
+++ b/solution.py
@@ -12,8 +12,16 @@
 HD = 64
 MESH = pl.DeviceIdType.MESH
 ROWS = 48
-SLOTS = 6
-EARLY = 2
+SLOTS = 4
+EARLY = 1
+MOST = 9
+PACK = 32
+STRIDE = 24
+CUTS = 3
+STRAIGHT = 1
+LATE = 1
+SMALL = -2
+GAP = 3
 
 
 def passed_along(block, axis, distance):
@@ -176,25 +184,29 @@
 
 
 class Reduction:
-    def __init__(self, depth, early, parts, total, scratch):
-        self.depth, self.early = depth, early
-        self.count, self.passes = parts.shape[0], parts.shape[0] + early
+    def __init__(self, depth, early, straight, cuts, count, spot, parts, total, scratch):
+        self.depth, self.early, self.cuts = depth, early, cuts
+        self.count, self.passes, self.spot = count, count + early, spot
+        self.chained, self.hops = self.passes - straight, early > 0
         self.parts, self.total = parts, total
         self.from_core, self.from_y, self.from_low, self.from_high = scratch[:4]
         self.core_s, self.core_r, self.y_s, self.y_r = scratch[4:8]
         self.up_s, self.up_r, self.down_s, self.down_r, self.free = scratch[8:13]
+        self.cut_y_s, self.cut_y_r, self.cut_s, self.cut_r = scratch[13:17]
         self.section = lax.axis_index("section")
         self.me = lax.axis_index("batch")
         self.z, self.y, self.core = self.me // 4, (self.me // 2) % 2, self.me % 2
 
-    def scratch(depth, early, count, wide):
+    def scratch(depth, early, cuts, count, wide):
         low, dma = lambda *shape: pltpu.VMEM(shape, jnp.bfloat16), pltpu.SemaphoreType.DMA
         return [
             low(min(count, SLOTS), 2 * depth * ROWS, wide),
             low((count - early) * depth * ROWS + early * ROWS, wide),
             low(count + early, (depth - 1) * ROWS, wide),
             low(count + early, (depth - 1) * ROWS, wide),
-        ] + [dma((count,))] * 4 + [dma((count + early, depth))] * 4 + [pltpu.SemaphoreType.REGULAR]
+        ] + [dma((count,))] * 4 + [dma((count + early, depth))] * 4 + [
+            pltpu.SemaphoreType.REGULAR, dma((cuts,)), dma((cuts,)), dma((cuts, depth)), dma((cuts, depth))
+        ]
 
     def device(self, z, y, core):
         return (self.section, z * 4 + y * 2 + core)
@@ -224,12 +236,12 @@
         pl.semaphore_wait(pltpu.get_barrier_semaphore(), self.depth + 2)
 
     def block(self, k, core, y, z):
-        return self.parts.at[k, rows_of(place(z, y, core, self.depth))]
+        return self.parts.at[self.spot(k), rows_of(place(z, y, core, self.depth))]
 
     def core_copy(self, k):
         half = 2 * self.depth * ROWS
         return pltpu.make_async_remote_copy(
-            self.parts.at[k, pl.ds(pl.multiple_of((1 - self.core) * half, half), half)],
+            self.parts.at[self.spot(k), pl.ds(pl.multiple_of((1 - self.core) * half, half), half)],
             self.from_core.at[k % SLOTS], self.core_s.at[k], self.core_r.at[k],
             device_id=self.peers()[0], device_id_type=MESH,
         )
@@ -244,13 +256,13 @@
         quarter = self.depth * ROWS
         start, slot = (self.core * 2 + 1 - self.y) * quarter, self.slot(k) * quarter
         return pltpu.make_async_remote_copy(
-            self.parts.at[k, pl.ds(pl.multiple_of(start, quarter), quarter)],
+            self.parts.at[self.spot(k), pl.ds(pl.multiple_of(start, quarter), quarter)],
             self.from_y.at[pl.ds(pl.multiple_of(slot, quarter), quarter)], self.y_s.at[k], self.y_r.at[k],
             device_id=self.peers()[1], device_id_type=MESH,
         )
 
     def last_rows(self, k):
-        return rows_of((self.count - self.early) * self.depth + k - 1)
+        return rows_of((MOST - self.early) * self.depth + k - 1)
 
     def last_copy(self, k):
         return pltpu.make_async_remote_copy(
@@ -305,9 +317,14 @@
 
             if far:
 
-                @pl.when(jnp.logical_not(self.is_early(k)))
+                @pl.when(jnp.logical_not(self.is_early(k)) & (k < self.count - 1))
                 def _():
                     self.y_copy(k).start()
+
+                @pl.when(k == self.count - 1)
+                def _():
+                    for cut in range(self.cuts):
+                        self.y_cut(cut).start()
 
         @pl.when(k + SLOTS < self.count)
         def _():
@@ -369,7 +386,9 @@
             @pl.when((p < 2 * self.early) & (p % 2 == 0))
             def _():
                 own[...] = total[...].astype(jnp.bfloat16)
-                self.last_copy(k).start()
+
+    def start_last(self, k):
+        self.last_copy(k).start()
 
     def after_last(self, k):
         self.last_copy(k).wait_recv()
@@ -379,7 +398,7 @@
         self.core_copy(k).wait_send()
         if self.early:
             pl.when(self.is_early(k))(lambda: self.last_copy(k).wait_send())
-        pl.when(jnp.logical_not(self.is_early(k)))(lambda: self.y_copy(k).wait_send())
+        pl.when(jnp.logical_not(self.is_early(k)) & (k < self.count - 1))(lambda: self.y_copy(k).wait_send())
 
     def drain_pass(self, p):
         for to in range(self.depth - 1):
@@ -392,19 +411,19 @@
             def _():
                 self.down_copy(p, to).wait_send()
 
-    def direct_copy(self, p, to):
+    def straight_copy(self, p, to):
         return pltpu.make_async_remote_copy(
             self.pass_block(p, to), self.from_low.at[p, rows_of(self.z - (self.z > to).astype(jnp.int32))],
             self.up_s.at[p, to], self.up_r.at[p, self.z],
             device_id=self.device(to, self.y, self.core), device_id_type=MESH,
         )
 
-    def go_direct(self, p):
+    def go_straight(self, p):
         for distance in range(self.depth - 1, 0, -1):
-            pl.when(self.z + distance < self.depth)(lambda: self.direct_copy(p, self.z + distance).start())
-            pl.when(self.z >= distance)(lambda: self.direct_copy(p, self.z - distance).start())
-
-    def finish_direct(self, p):
+            pl.when(self.z + distance < self.depth)(lambda: self.straight_copy(p, self.z + distance).start())
+            pl.when(self.z >= distance)(lambda: self.straight_copy(p, self.z - distance).start())
+
+    def finish_straight(self, p):
         k, _ = self.of_pass(p)
         total = self.total.at[rows_of(k)]
         total[...] = self.pass_block(p, self.z)[...].astype(jnp.float32)
@@ -419,24 +438,89 @@
             ).wait_recv()
             total[...] += arrived[...].astype(jnp.float32)
 
-    def drain_direct(self, p):
+    def drain_straight(self, p):
         for to in range(self.depth):
-            pl.when(self.z != to)(lambda: self.direct_copy(p, to).wait_send())
+            pl.when(self.z != to)(lambda: self.straight_copy(p, to).wait_send())
+
+    def columns(self, cut):
+        wide = self.parts.shape[2] // self.cuts
+        return pl.ds(pl.multiple_of(cut * wide, wide), wide)
+
+    def y_cut(self, cut):
+        quarter, columns = self.depth * ROWS, self.columns(cut)
+        start, slot = (self.core * 2 + 1 - self.y) * quarter, (self.count - 1 - self.early) * quarter
+        return pltpu.make_async_remote_copy(
+            self.parts.at[self.spot(self.count - 1), pl.ds(pl.multiple_of(start, quarter), quarter), columns],
+            self.from_y.at[pl.ds(pl.multiple_of(slot, quarter), quarter), columns], self.cut_y_s.at[cut], self.cut_y_r.at[cut],
+            device_id=self.peers()[1], device_id_type=MESH,
+        )
+
+    def cut_block(self, to, cut):
+        rows = rows_of(place(to, self.y, self.core, self.depth))
+        return self.parts.at[self.spot(self.count - 1), rows, self.columns(cut)]
+
+    def direct_copy(self, to, cut):
+        rows = rows_of(self.z - (self.z > to).astype(jnp.int32))
+        return pltpu.make_async_remote_copy(
+            self.cut_block(to, cut), self.from_low.at[self.passes - 1, rows, self.columns(cut)],
+            self.cut_s.at[cut, to], self.cut_r.at[cut, self.z],
+            device_id=self.device(to, self.y, self.core), device_id_type=MESH,
+        )
+
+    def go_direct(self):
+        @pl.loop(0, self.cuts)
+        def _(cut):
+            self.y_cut(cut).wait_recv()
+            columns, first = self.columns(cut), (self.count - 1 - self.early) * self.depth
+
+            @pl.loop(0, self.depth)
+            def _(to):
+                self.add(self.cut_block(to, cut), self.from_y[rows_of(first + to), columns])
+
+            for distance in range(self.depth - 1, 0, -1):
+                pl.when(self.z + distance < self.depth)(lambda: self.direct_copy(self.z + distance, cut).start())
+                pl.when(self.z >= distance)(lambda: self.direct_copy(self.z - distance, cut).start())
+
+    def finish_direct(self):
+        @pl.loop(0, self.cuts)
+        def _(cut):
+            total = self.total.at[rows_of(self.count - 1), self.columns(cut)]
+            total[...] = self.cut_block(self.z, cut)[...].astype(jnp.float32)
+
+            @pl.loop(0, self.depth - 1)
+            def _(i):
+                source = i + (i >= self.z).astype(jnp.int32)
+                arrived = self.from_low.at[self.passes - 1, rows_of(i), self.columns(cut)]
+                pltpu.make_async_remote_copy(
+                    arrived, arrived, self.cut_s.at[cut, source], self.cut_r.at[cut, source],
+                    device_id=self.device(source, self.y, self.core), device_id_type=MESH,
+                ).wait_recv()
+                total[...] += arrived[...].astype(jnp.float32)
+
+    def drain_direct(self):
+        @pl.loop(0, self.cuts)
+        def _(cut):
+            self.y_cut(cut).wait_send()
+            for to in range(self.depth):
+                pl.when(self.z != to)(lambda: self.direct_copy(to, cut).wait_send())
 
     def along(self, t, ahead):
-        last, soon, chained = self.depth - 1, 2 * self.early, self.passes - 1
-        for far, action in ((self.z, self.go_up), (last - self.z, self.go_down)) if chained else ():
+        last, soon, chained = self.depth - 1, 2 * self.early, self.chained
+        for far, action in ((self.z, self.go_up), (last - self.z, self.go_down)) if self.hops else ():
             pl.when(far > 0)(lambda far=far, action=action: at(t - far, 0, chained, action))
 
         ends = ((self.z == 0, self.go_up), (self.z == last, self.go_down))
         for end, action in ends:
             if self.early:
                 pl.when(end)(lambda action=action: at(t + ahead, 0, soon, action))
-        at(t, soon, self.passes, self.after_y)
+        if self.hops:
+            at(t, soon, self.passes - 1, self.after_y)
         for end, action in ends:
-            if chained:
+            if self.hops:
                 pl.when(end)(lambda action=action: at(t, soon, chained, action))
-        at(t, chained, self.passes, self.go_direct)
+        if self.hops:
+            at(t, chained, self.passes - 1, self.go_straight)
+        pl.when(t == self.passes - 1)(self.go_direct)
 
 
 def at(k, low, high, action):
@@ -456,20 +540,30 @@
 
 def train_kernel(
     depth, images,
-    patches, signs, tiles, valid, cotangent, attend_in, project_in, expand_in, shrink_in, first, second, bottle_in,
-    results, total, rest,
-    parts, attend, project, left, right, soft, temp, saved, normed_one, normed_two, residual, factor_one,
-    factor_two, average_two, bias, codes, bottle, delta, code_grad, bottle_sum, gain_one, gain_two, extra,
-    loads, code_sems, *scratch,
+    patches, signs_in, tiles_in, valid_in, cotangent, attend_in, project_in, expand_in, shrink_in, first_in, second_in,
+    bottle_from, results, total_out, rest_out,
+    signs, tiles, valid, first, second, bottle_in, rest, total, parts, attend, project, left, right, soft, temp, saved, normed_one, normed_two, residual, factor_one,
+    factor_two, average_two, bias, codes, bottle, delta, code_grad, bottle_sum, mix, packed, code_sum,
+    code_core, code_y, code_z, code_other, gain_one, gain_two, extra,
+    loads, code_sems, stores, sum_sems, *scratch,
 ):
     rows, width = patches.shape
     length = rows // images
     work = total.at[:rows]
     count, slabs = parts.shape[0], shrink_in.shape[0] // width
     pairs = width // 128
-    main = Reduction(depth, EARLY, parts, total, scratch[:13])
-    small = Reduction(depth, 0, extra, rest, scratch[13:26])
-    encoding = main.section == 0
+    encoding = lax.axis_index("section") == 0
+
+    def content(k):
+        other = jnp.where(k < 2 * slabs, (k + slabs) % (2 * slabs), k)
+        return jnp.where(encoding, (k + slabs) % count, other)
+
+    def location(k):
+        return (k + jnp.where(encoding, slabs, 2 * slabs)) % count
+
+    held = jnp.where(encoding, slabs + 4, 2 * slabs + 1)
+    main = Reduction(depth, EARLY, STRAIGHT, CUTS, held, location, parts, total, scratch[:17])
+    small = Reduction(depth, 0, 1, 1, 1, lambda k: k, extra, rest, scratch[17:34])
     lane = lax.broadcasted_iota(jnp.int32, (length, 128), 1)
     low_half = lane < HD
     bf, f32 = jnp.bfloat16, jnp.float32
@@ -480,29 +574,47 @@
     def load(source, target, i):
         return pltpu.make_async_copy(source, target, loads.at[i])
 
-    main.greet()
+    little = [
+        load(source, target, 7 + 2 * slabs + i)
+        for i, (source, target) in enumerate(
+            (
+                (signs_in, signs), (bottle_from, bottle_in), (tiles_in, tiles), (valid_in, valid), (first_in, first),
+                (second_in, second),
+            )
+        )
+    ]
+    for copy in little[:2]:
+        copy.start()
     fetch = [load(patches, right.at[5], 0)]
     fetch += [load(attend_in.at[:, pl.ds(j * width, width)], attend.at[j], 1 + j) for j in range(3)]
-    for copy in fetch:
+    for copy in fetch + little[2:]:
         copy.start()
+    main.greet()
     fetch += [load(project_in, project, 4)]
     fetch += [load(expand_in.at[:, pl.ds(j * width, width)], parts.at[2 * slabs + j], 5 + j) for j in range(slabs)]
     fetch += [load(shrink_in.at[pl.ds(j * width, width)], parts.at[slabs + j], 5 + slabs + j) for j in range(slabs)]
     fetch += [load(cotangent, right.at[0], 5 + 2 * slabs)]
 
-    for i in range(images):
-        row = jnp.broadcast_to(tiles[i : i + 1, :].astype(f32), (length, length))
-        live = jnp.broadcast_to(valid[i : i + 1, :], (length, length)) == 1
-        spot = lax.broadcasted_iota(jnp.int32, (length, length), 0) == lax.broadcasted_iota(
-            jnp.int32, (length, length), 1
-        )
-        bias[i] = jnp.where(((row == row.T) & live) | spot, 0.0, -1000000000.0)
+    for copy in little[:2]:
+        copy.wait()
     code_width = signs.shape[0]
     work[:256, :] = jnp.zeros((256, width), f32)
     work[:code_width, :rows] = (2 * signs[...] - 1).astype(f32) / math.sqrt(code_width)
     work[128 : 128 + code_width, :] = bottle_in[...].astype(f32)
     codes[...] = work[:128, :rows].T.astype(bf)
     bottle[...] = work[128:256, :].T.astype(bf)
+    for copy in little[2:]:
+        copy.wait()
+    for i in range(images):
+        row = jnp.broadcast_to(tiles[i : i + 1, :].astype(f32), (length, length))
+        live = jnp.broadcast_to(valid[i : i + 1, :], (length, length)) == 1
+        spot = lax.broadcasted_iota(jnp.int32, (length, length), 0) == lax.broadcasted_iota(
+            jnp.int32, (length, length), 1
+        )
+        bias[i] = jnp.where(((row == row.T) & live) | spot, 0.0, -1000000000.0)
+    turned = work[128:256, :]
+    mix[...] = ((turned - jnp.mean(turned, axis=1, keepdims=True)) * first[...]).T.astype(bf)
+    packed[...] = jnp.zeros_like(packed)
     gain_one[...] = jnp.zeros_like(gain_one)
     gain_two[...] = jnp.zeros_like(gain_two)
     fetch[0].wait()
@@ -545,7 +657,6 @@
                 copy.start()
         right[6 + j] = dot(temp[...], attend[j]).astype(bf)
 
-    keep_transpose(temp, left.at[slabs + 2])
 
     group = 3
     heads = [(pair, head) for pair in range(group) for head in range(2)]
@@ -583,7 +694,6 @@
 
     keep_transpose(temp, left.at[slabs + 1])
     norm(second, normed_two, factor_two, average_two)
-    keep_transpose(temp, left.at[slabs])
 
     for j in range(slabs):
         fetch[5 + j].wait()
@@ -605,6 +715,10 @@
     @pl.when(jnp.logical_not(encoding))
     def _():
         residual[...] = right[0].astype(f32)
+
+    def keep_norm(gain, normed, target):
+        temp[...] = (normed[...] * gain[...]).astype(bf)
+        keep_transpose(temp, target)
 
     def block_output():
         output = normed_two[...] * (1.0 / factor_two[...]) + average_two[...]
@@ -634,13 +748,13 @@
         grad_out = times_transpose(grad_latent, bottle[...])
         right[0] = grad_out.astype(bf)
         residual[...] = grad_out
-        bottle_sum[...] = contract_rows(saved[...], grad_latent)
+        codes[...] = grad_latent
 
     def piece(k):
-        a = jnp.minimum(k, slabs) + (k >= 2 * slabs).astype(jnp.int32) + (k > 2 * slabs).astype(jnp.int32)
-        b = jnp.maximum(k - slabs + 1, 0)
-
-        parts[k] = dot(left[a], right[b]).astype(bf)
+        c = content(k)
+        a = jnp.minimum(c, slabs) + (c >= 2 * slabs).astype(jnp.int32) + (c > 2 * slabs).astype(jnp.int32)
+        b = jnp.maximum(c - slabs + 1, 0)
+        parts[location(k)] = dot(left[a], right[b]).astype(bf)
         main.start(k)
 
     def norm_back(gain, normed, factor, gain_sum, low):
@@ -694,11 +808,89 @@
                 right[7, r, c] = (to_key[2 * pair] + to_key[2 * pair + 1]).astype(bf)
                 right[8, r, c] = (to_value[2 * pair] + to_value[2 * pair + 1]).astype(bf)
 
+    half = 3 * width // 2
+    own_half = pl.ds(pl.multiple_of(main.core * half, half), half)
+
+    def sum_copy(stage, source, target, send, receive, device):
+        return pltpu.make_async_remote_copy(
+            source, target, sum_sems.at[2 * stage, send], sum_sems.at[2 * stage + 1, receive],
+            device_id=device, device_id_type=MESH,
+        )
+
+    def sum_core():
+        return sum_copy(0, code_sum, code_core, 0, 0, main.peers()[0])
+
+    def sum_y():
+        return sum_copy(0, code_sum.at[:, own_half], code_y, 1, 1, main.peers()[1])
+
+    def sum_back():
+        return sum_copy(0, code_sum.at[:, own_half], code_other, 2, 2, main.peers()[0])
+
+    def sum_z(to):
+        return sum_copy(
+            1, code_sum.at[:, own_half], code_z.at[main.z - (main.z > to).astype(jnp.int32)], to, main.z,
+            main.device(to, main.y, main.core),
+        )
+
+    def sum_codes():
+        scaled = (codes[...].astype(f32) * factor_one[...]).astype(bf)
+        for j in range(3):
+            code_sum[:, j * width : (j + 1) * width] = contract_rows(scaled, right[6 + j])[: code_sum.shape[0]].astype(bf)
+        sum_core().start()
+
+    def sum_after_core():
+        sum_core().wait_send()
+        sum_core().wait_recv()
+        code_sum[...] = (code_sum[...].astype(f32) + code_core[...].astype(f32)).astype(bf)
+        sum_y().start()
+
+    def sum_after_y():
+        sum_y().wait_send()
+        sum_y().wait_recv()
+        code_sum[:, own_half] = (code_sum[:, own_half].astype(f32) + code_y[...].astype(f32)).astype(bf)
+        for to in range(depth):
+            pl.when(main.z != to)(lambda: sum_z(to).start())
+
+    def sum_after_z():
+        together = code_sum[:, own_half].astype(f32)
+        for z in range(depth):
+            pl.when(main.z != z)(lambda: sum_z(z).wait_send())
+            source = code_z.at[jnp.minimum(z, depth - 2)]
+
+            @pl.when(main.z != z)
+            def _():
+                sum_copy(1, source, source, z, z, main.device(z, main.y, main.core)).wait_recv()
+
+        for i in range(depth - 1):
+            together += code_z[i].astype(f32)
+        code_sum[:, own_half] = together.astype(bf)
+        sum_back().start()
+
+    def finish_attend():
+        sum_back().wait_send()
+        sum_back().wait_recv()
+        code_sum[:, pl.ds(pl.multiple_of((1 - main.core) * half, half), half)] = code_other[...]
+        own = mix[pl.ds(pl.multiple_of(main.me * ROWS, ROWS), ROWS), :][:, : code_sum.shape[0]]
+        for j in range(3):
+            k = 2 * slabs + 1 + j
+            total[k * ROWS : (k + 1) * ROWS, :] = dot(own, code_sum[:, j * width : (j + 1) * width])
+            store(k).start()
+
     def through_attend():
         grad = times_transpose(right[6], attend[0])
         for j in range(1, 3):
             grad += times_transpose(right[6 + j], attend[j])
         work[...] = grad
+
+        @pl.when(encoding)
+        def _():
+            bottle_sum[...] = contract_rows(saved[...], codes[...])
+            latent = codes[...].astype(f32)
+            together = dot(left[0], pltpu.roll(latent, PACK, 1).astype(bf))
+            for j in range(1, slabs):
+                together += dot(left[j], pltpu.roll(latent, PACK + STRIDE * j, 1).astype(bf))
+            packed[...] = together
+
         norm_back(first, normed_one, factor_one, gain_one, saved)
 
         @pl.when(jnp.logical_not(encoding))
@@ -707,6 +899,7 @@
             delta[...] = turned[: delta.shape[0]].astype(bf)
             across.start()
             bottle_sum[...] = contract_rows(saved[...], codes[...])
+            sum_codes()
 
         @pl.when(encoding)
         def _():
@@ -717,53 +910,112 @@
         column_two = jnp.sum(gain_two[...].T, axis=1, keepdims=True)
         gathered = jnp.where(
             spare == code_width, column_one, jnp.where(spare == code_width + 1, column_two, bottle_sum[...])
-        ).astype(bf)
+        )
         for i in range(4 * depth):
-            spot = place(i // 4, (i // 2) % 2, i % 2, depth)
-            extra[0, spot * ROWS : (spot + 1) * ROWS, :] = gathered[i * ROWS : (i + 1) * ROWS]
+            start = place(i // 4, (i // 2) % 2, i % 2, depth) * ROWS
+            extra[0, start : start + ROWS, :] = (
+                gathered[i * ROWS : (i + 1) * ROWS] + packed[start : start + ROWS, :]
+            ).astype(bf)
         small.start(0)
 
-    turns = images * pairs // group
-    links, within, last = 6, slabs, depth - 1
-
-    @pl.loop(0, links + main.passes + slabs + 6)
+    def store(k):
+        return pltpu.make_async_copy(total.at[rows_of(k)], total_out.at[rows_of(content(k))], stores.at[k])
+
+    def finish(p):
+        main.finish(p)
+        piece, _ = main.of_pass(p)
+        pl.when(p >= 2 * EARLY)(store(piece).start)
+
+    def finish_straight(p):
+        main.finish_straight(p)
+        store(main.of_pass(p)[0]).start()
+
+    def finish_early(k):
+        main.after_last(k)
+        store(k).start()
+
+    rest_copy = pltpu.make_async_copy(rest, rest_out, loads.at[13 + 2 * slabs])
+
+    def finish_small():
+        small.finish_direct()
+        rest_copy.start()
+
+        @pl.when(encoding)
+        def _():
+            for j in range(slabs):
+                exact = pltpu.roll(rest[...], 128 - PACK - STRIDE * j, 1)
+                high = exact.astype(bf)
+                low = (exact - high.astype(f32)).astype(bf)
+                k = slabs + 4 + j
+                total[k * ROWS : (k + 1) * ROWS, :] = times_transpose(high, bottle[...]) + times_transpose(low, bottle[...])
+                store(k).start()
+
+    def send_late():
+        for k in range(1 + EARLY - LATE, 1 + EARLY):
+            main.start_last(k)
+
+    def finish_last():
+        main.finish_direct()
+        store(held - 1).start()
+
+    turns, links = images * pairs // group, 6
+
+    @pl.loop(0, links + MOST + EARLY + 10)
     def _(step):
         k = step - links * main.section
-        link = step - within * (1 - main.section)
-        pl.when(k == 0)(block_output)
+        link = jnp.where(encoding, jnp.where(step == 0, 0, jnp.where(step >= 3, step - 2, -1)), step)
+        pl.when((k == 0) & encoding)(lambda: keep_norm(first, normed_one, left.at[slabs + 2]))
+        pl.when(k == 0)(lambda: keep_norm(second, normed_two, left.at[slabs]))
+        pl.when(k == slabs * main.section)(block_output)
         pl.when((k == 0) & encoding)(from_codes)
-        at(k - (k > slabs).astype(jnp.int32), 0, jnp.where(k == slabs, 0, count), piece)
-        at(k - 2, 0, count, main.after_core)
-        at(k - slabs - 6, 0, 1, small.after_core)
+        pl.when(link == 0)(through_shrink)
+        now = jnp.where(k < slabs, k, jnp.where(k == slabs + 1, slabs, jnp.where(k >= slabs + 3, k - 2, -1)))
+        at(now, 0, held, piece)
+        met = jnp.where(k <= slabs + 2, k - 2, jnp.where(k >= slabs + 4, k - 3, -1))
+        at(met, 0, held, main.after_core)
         main.along(k - 5, 2)
-        small.along(k - slabs - 12, 0)
-        at(k - 10, 0, main.passes - 1, main.finish)
-        at(k - 10, main.passes - 1, main.passes, main.finish_direct)
-        at(k - slabs - 16, 0, 1, small.finish_direct)
-        at(k - 15, 1, 1 + EARLY, main.after_last)
-        pl.when(link == 0)(through_shrink)
+        at(k - 10, 0, main.chained, finish)
+        at(k - 10, main.chained, main.passes - 1, finish_straight)
+        pl.when(k == main.passes + 9)(finish_last)
+        at(k - 12, 1, 1 + EARLY - LATE, main.start_last)
+        at(k - slabs - SMALL - 6, 0, 1, small.after_core)
+        small.along(k - slabs - SMALL - 7 - GAP, 0)
+        pl.when(k == main.passes + 4)(send_late)
+        pl.when(k == slabs + SMALL + GAP + 8)(finish_small)
+        at(k - main.passes - 7, 1, 1 + EARLY, finish_early)
+        for moment, action in ((2, sum_after_core), (7, sum_after_y), (9, sum_after_z), (11, finish_attend)):
+            pl.when(jnp.logical_not(encoding) & (k == moment))(action)
         pl.when(link == 1)(through_expand)
         pl.when(link == 2)(through_project)
         pl.when((link == 3) | (link == 4))(lambda: through_heads((link - 3) * turns // 2, (link - 2) * turns // 2))
         pl.when(link == 5)(through_attend)
 
     out_copy.wait()
+    rest_copy.wait()
 
     @pl.when(jnp.logical_not(encoding))
     def _():
         across.wait_send()
 
     small.drain(0)
-    small.drain_direct(0)
-    main.drain_direct(main.passes - 1)
+    small.drain_direct()
+    main.drain_direct()
+
+    @pl.loop(0, held)
+    def _(k):
+        main.drain(k)
 
     @pl.loop(0, count)
     def _(k):
-        main.drain(k)
-
-    @pl.loop(0, main.passes - 1)
+        store(k).wait()
+
+    @pl.loop(0, main.chained)
     def _(p):
         main.drain_pass(p)
+
+    @pl.loop(main.chained, main.passes - 1)
+    def _(p):
+        main.drain_straight(p)
 
 
 def train(depth, images, arrays):
@@ -773,7 +1025,7 @@
     count = 2 * slabs + 4
     pairs, length = width // 128, rows // images
     code_rows = -(-signs.shape[0] // 16) * 16
-    hbm, vmem = pl.BlockSpec(memory_space=pl.ANY), pl.BlockSpec(memory_space=pltpu.VMEM)
+    hbm = pl.BlockSpec(memory_space=pl.ANY)
     low, full = lambda *shape: pltpu.VMEM(shape, jnp.bfloat16), lambda *shape: pltpu.VMEM(shape, jnp.float32)
     return pl.pallas_call(
         functools.partial(train_kernel, depth, images),
@@ -782,9 +1034,12 @@
             jax.ShapeDtypeStruct((count * ROWS, width), jnp.float32),
             jax.ShapeDtypeStruct((ROWS, 128), jnp.float32),
         ),
-        in_specs=[hbm, vmem, vmem, vmem, hbm, hbm, hbm, hbm, hbm, vmem, vmem, vmem],
-        out_specs=[hbm, vmem, vmem],
-        scratch_shapes=[
+        in_specs=[hbm] * 12,
+        out_specs=[hbm] * 3,
+        scratch_shapes=[pltpu.VMEM(arrays[i].shape, arrays[i].dtype) for i in (1, 2, 3, 9, 10, 11)]
+        + [
+            full(ROWS, 128),
+            full(count * ROWS, width),
             low(count, width, width),
             low(3, width, width),
             low(width, width),
@@ -805,14 +1060,23 @@
             low(code_rows, rows),
             low(code_rows, rows),
             full(width, 128),
+            low(width, 128),
+            full(width, 128),
+            low(code_rows, 3 * width),
+            low(code_rows, 3 * width),
+            low(code_rows, 3 * width // 2),
+            low(depth - 1, code_rows, 3 * width // 2),
+            low(code_rows, 3 * width // 2),
             full(8, width),
             full(8, width),
             low(1, width, 128),
-            pltpu.SemaphoreType.DMA((7 + 2 * slabs,)),
+            pltpu.SemaphoreType.DMA((14 + 2 * slabs,)),
             pltpu.SemaphoreType.DMA((2,)),
+            pltpu.SemaphoreType.DMA((count,)),
+            pltpu.SemaphoreType.DMA((6, depth)),
         ]
-        + Reduction.scratch(depth, EARLY, count, width)
-        + Reduction.scratch(depth, 0, 1, 128),
+        + Reduction.scratch(depth, EARLY, CUTS, MOST, width)
+        + Reduction.scratch(depth, 0, 1, 1, 128),
         compiler_params=pltpu.CompilerParams(collective_id=0, has_side_effects=True, vmem_limit_bytes=63 << 20),
         name="train",
     )(*arrays)

time: 128 us -> 112 us (0.88)
  Pallas kernels: 127 us -> 111 us
    pallas_call x1, Pallas kernels: 124 us -> 108 us  [train(): pl.pallas_call(functools.partial(train_kernel, depth, images), out_shape=...]
where the time goes in v3:
time: 112 us; the launch traced here: 111 us
  Pallas kernels  111 us (99%)
    pallas_call x1, Pallas kernels, train(): pl.pallas_call(functools.partial(train_kernel, depth, images), out_shape=...  108 us
    pallas_call x1, Pallas kernels, deliver(): pl.pallas_call(functools.partial(deliver_kernel, slabs, code), out_shape=...  3.17 us

profile of v3, /device:TPU:0, one launch (start us, length us, event | category | flops | bytes accessed | tf_op | source)
XLA Modules:
  0.0 111.4 jit_solution(9924691531283728153)
XLA Ops:
  0.6 107.6 %train.1 = (bf16[512,768]{1,0:T(8,128)(2,1)}, f32[576,768]{1,0:T(8,128)}, f32[48,128]{1,0:T(8,128)}) custom-call(bf16[512,768]{1,0:T(8,128)(2,1)} %patches.1, s32[18,512]{1,0:T(8,128)} %bitcast.18, s32[2,256]{1,0:T(2,128)} %tiles_in.1, s32[2,256]{1,0:T(2,128)} %valid_in.1, bf16[512,768]{1,0:T(8,128)(2,1)} %cotangent.1, bf16[768,2304]{1,0:T(8,128)(2,1)} %bitcast.16, ...), custom_call_target="tpu_custom_call" | custom-call | tf_op jit(solution)/shard_map/train/pallas_call | solution.py:1030
  108.2 3.2 %deliver.1 = (bf16[512,768]{1,0:T(8,128)(2,1)}, f32[48,2304]{1,0:T(8,128)}, f32[48,768]{1,0:T(8,128)}, f32[48,3072]{1,0:T(8,128)}, f32[192,768]{1,0:T(8,128)}, /...) custom-call(bf16[512,768]{1,0:T(8,128)(2,1)} %get-tuple-element.19.raw, ...), custom_call_target="tpu_custom_call" | custom-call | tf_op jit(solution)/shard_map/deliver/pallas_call | solution.py:1106

commit v4 on v3

--- a/solution.py
+++ b/solution.py
@@ -658,7 +658,7 @@
         right[6 + j] = dot(temp[...], attend[j]).astype(bf)
 
 
-    group = 3
+    group = 6
     heads = [(pair, head) for pair in range(group) for head in range(2)]
 
     def group_of(turn):
@@ -768,8 +768,9 @@
             residual[r, :] = grad
             low[r, :] = grad.astype(bf)
 
-    def through_shrink():
-        for j in range(slabs):
+    def through_shrink(low, high):
+        @pl.loop(low, high)
+        def _(j):
             grad = times_transpose(right[0], parts[slabs + j])
             right[1 + j] = (grad * right[1 + j].astype(f32)).astype(bf)
 
@@ -898,12 +899,16 @@
             turned = lax.dot_general(bottle[...], saved[...], (((0,), (1,)), ((), ())), preferred_element_type=f32)
             delta[...] = turned[: delta.shape[0]].astype(bf)
             across.start()
-            bottle_sum[...] = contract_rows(saved[...], codes[...])
-            sum_codes()
 
         @pl.when(encoding)
         def _():
             out_copy.start()
+
+    def small_sums():
+        @pl.when(jnp.logical_not(encoding))
+        def _():
+            bottle_sum[...] = contract_rows(saved[...], codes[...])
+            sum_codes()
 
         spare = lax.broadcasted_iota(jnp.int32, (width, 128), 1)
         column_one = jnp.sum(gain_one[...].T, axis=1, keepdims=True)
@@ -963,12 +968,14 @@
     @pl.loop(0, links + MOST + EARLY + 10)
     def _(step):
         k = step - links * main.section
-        link = jnp.where(encoding, jnp.where(step == 0, 0, jnp.where(step >= 3, step - 2, -1)), step)
+        link = jnp.where(encoding, jnp.where(step >= 3, step - 2, -1), step)
         pl.when((k == 0) & encoding)(lambda: keep_norm(first, normed_one, left.at[slabs + 2]))
         pl.when(k == 0)(lambda: keep_norm(second, normed_two, left.at[slabs]))
         pl.when(k == slabs * main.section)(block_output)
         pl.when((k == 0) & encoding)(from_codes)
-        pl.when(link == 0)(through_shrink)
+        pl.when(jnp.where(encoding, step < slabs, step == 0))(
+            lambda: through_shrink(jnp.where(encoding, step, 0), jnp.where(encoding, step + 1, slabs))
+        )
         now = jnp.where(k < slabs, k, jnp.where(k == slabs + 1, slabs, jnp.where(k >= slabs + 3, k - 2, -1)))
         at(now, 0, held, piece)
         met = jnp.where(k <= slabs + 2, k - 2, jnp.where(k >= slabs + 4, k - 3, -1))
@@ -983,12 +990,13 @@
         pl.when(k == main.passes + 4)(send_late)
         pl.when(k == slabs + SMALL + GAP + 8)(finish_small)
         at(k - main.passes - 7, 1, 1 + EARLY, finish_early)
-        for moment, action in ((2, sum_after_core), (7, sum_after_y), (9, sum_after_z), (11, finish_attend)):
+        for moment, action in ((5, sum_after_core), (8, sum_after_y), (10, sum_after_z), (12, finish_attend)):
             pl.when(jnp.logical_not(encoding) & (k == moment))(action)
         pl.when(link == 1)(through_expand)
         pl.when(link == 2)(through_project)
         pl.when((link == 3) | (link == 4))(lambda: through_heads((link - 3) * turns // 2, (link - 2) * turns // 2))
         pl.when(link == 5)(through_attend)
+        pl.when(k == jnp.where(encoding, 7, 3))(small_sums)
 
     out_copy.wait()
     rest_copy.wait()

time: 112 us -> 112 us (level)
  no operation moved by 1% of the time
where the time goes in v4:
time: 112 us
  Pallas kernels  111 us (99%)
    pallas_call x1, Pallas kernels, train(): pl.pallas_call(functools.partial(train_kernel, depth, images), out_shape=...  108 us
    pallas_call x1, Pallas kernels, deliver(): pl.pallas_call(functools.partial(deliver_kernel, slabs, code), out_shape=...  3.17 us

profile of v4, /device:TPU:0, one launch (start us, length us, event | category | flops | bytes accessed | tf_op | source)
XLA Modules:
  0.0 111.6 jit_solution(2888737817015440356)
XLA Ops:
  0.6 107.8 %train.1 = (bf16[512,768]{1,0:T(8,128)(2,1)}, f32[576,768]{1,0:T(8,128)}, f32[48,128]{1,0:T(8,128)}) custom-call(bf16[512,768]{1,0:T(8,128)(2,1)} %patches.1, s32[18,512]{1,0:T(8,128)} %bitcast.18, s32[2,256]{1,0:T(2,128)} %tiles_in.1, s32[2,256]{1,0:T(2,128)} %valid_in.1, bf16[512,768]{1,0:T(8,128)(2,1)} %cotangent.1, bf16[768,2304]{1,0:T(8,128)(2,1)} %bitcast.16, ...), custom_call_target="tpu_custom_call" | custom-call | tf_op jit(solution)/shard_map/train/pallas_call | solution.py:1038
  108.4 3.2 %deliver.1 = (bf16[512,768]{1,0:T(8,128)(2,1)}, f32[48,2304]{1,0:T(8,128)}, f32[48,768]{1,0:T(8,128)}, f32[48,3072]{1,0:T(8,128)}, f32[192,768]{1,0:T(8,128)}, /...) custom-call(bf16[512,768]{1,0:T(8,128)(2,1)} %get-tuple-element.19.raw, ...), custom_call_target="tpu_custom_call" | custom-call | tf_op jit(solution)/shard_map/deliver/pallas_call | solution.py:1114
